TPU v7x, 128 devices: a whole 4x4x4 slice. The times are simulated.
128 devices in a mesh: dp: 16 (over x, z_hi, core), fsdp: 8 (over y, z_lo).
Axes of the slice: x: 4, y: 4, z: 4 (z_hi: 2, z_lo: 2; z = z_hi * 2 + z_lo), core: 2. Of those that a mesh axis runs over, the one named last changes fastest.
Arguments:
- frames: bfloat16 [65536, 2048], P(('dp', 'fsdp')), may hold values from -120 to 120, as said below
- bounds: int32 [2, 65536], P(None, ('dp', 'fsdp')), may hold values from -1 to 399, as said below
- destinations: int32 [16, 8, 16], P(None, 'fsdp'), may hold values from -1 to 15, as said below
- kernel: float32 [9, 2048], replicated, may hold values from -2 to 2
- norm_gain: float32 [2048], replicated, may hold values from 0.5 to 2
- norm_shift: float32 [2048], replicated, may hold values from -3 to 3
- panel: bfloat16 [2048, 2048], P('fsdp'), may hold values from -0.125 to 0.125
- cotangent: bfloat16 [49152, 2048], P(('dp', 'fsdp')), may hold values from -6 to 6
Outputs:
- mapped: bfloat16 [49152, 2048], P(('dp', 'fsdp'))
- input_grad: bfloat16 [65536, 2048], P(('dp', 'fsdp'))
- panel_grad: float32 [2048, 2048], P('fsdp')
- kernel_grad: float32 [9, 2048], replicated
- norm_grads: float32 [2, 2048], replicated
Inputs may be any that keep to these rules, and one draw needn't show every extreme that they name: `bounds`: A frame's count of earlier and later frames of its utterance along the stream of live frames; both are -1 on padding frames, which fill each device's last blocks; every device has a multiple of 32 live frames, the same ones that destinations marks live. Utterances hold at most 400 frames, and one holds exactly 400. destinations[d, f, b] is the data index in column f that receives block b of device (d, f), or -1 for a padding block. A device's live blocks come first and number from 8 to 16; a device sends at most one block to each device of its column, and every device receives exactly 12 blocks. Input features; padding frames hold arbitrary values.
All inputs are finite; a program needn't handle non-finite values.
Results may differ from a plain program's by a relative error of at most 0.005.
Values may be sent and summed in bfloat16 or wider, within the bound.
A program may use at most 128 MiB of HBM per device.

v0:
```python
import jax
import jax.numpy as jnp
from jax import lax
from jax.sharding import PartitionSpec as P

BLOCK_FRAMES = 32


epsilon = 1e-05


def with_halo(block, sides, width):
    for axis, dim in sides:
        count = lax.axis_size(axis)
        forward = [(i, i + 1) for i in range(count - 1)]
        backward = [(target, source) for source, target in forward]
        low = lax.ppermute(
            lax.slice_in_dim(block, block.shape[dim] - width, None, axis=dim), axis, forward
        )
        high = lax.ppermute(lax.slice_in_dim(block, 0, width, axis=dim), axis, backward)
        block = jnp.concatenate([low, block, high], axis=dim)
    return block


def tap_mask(before_rows, after_rows, offset):
    return (before_rows >= max(-offset, 0)) & (after_rows >= max(offset, 0))


def conv_rows(extended, kernel, before_rows, after_rows):
    half_span = kernel.shape[0] // 2
    length = before_rows.shape[0]
    accum = jnp.zeros((length, extended.shape[1]), jnp.float32)
    for tap_index in range(kernel.shape[0]):
        offset = tap_index - half_span
        window = extended[tap_index : tap_index + length].astype(jnp.float32) * kernel[tap_index]
        accum = accum + jnp.where(tap_mask(before_rows, after_rows, offset)[:, None], window, 0.0)
    return accum


def conv_back(extended, kernel, before_rows, after_rows):
    half_span = kernel.shape[0] // 2
    length = before_rows.shape[0]
    accum = jnp.zeros((length, extended.shape[1]), jnp.float32)
    for tap_index in range(kernel.shape[0]):
        offset = tap_index - half_span
        first_row = 2 * half_span - tap_index
        window = extended[first_row : first_row + length] * kernel[tap_index]
        accum = accum + jnp.where(tap_mask(before_rows, after_rows, -offset)[:, None], window, 0.0)
    return accum


def kernel_terms(extended, gradient, before_rows, after_rows, kernel_taps):
    half_span = kernel_taps // 2
    length = before_rows.shape[0]
    tap_sums = []
    for tap_index in range(kernel_taps):
        offset = tap_index - half_span
        window = extended[tap_index : tap_index + length].astype(jnp.float32)
        masked = jnp.where(
            tap_mask(before_rows, after_rows, offset)[:, None], window * gradient, 0.0
        )
        tap_sums.append(jnp.sum(masked, axis=0))
    return jnp.stack(tap_sums)


def rim_rows(values, live_rows, half_span):
    leading = values[:half_span]
    trailing = lax.dynamic_slice_in_dim(values, live_rows - half_span, half_span, 0)
    return jnp.concatenate([leading, trailing], axis=0)


def extend(values, previous, following, live_rows):
    half_span = previous.shape[0]
    padding = jnp.zeros((half_span, values.shape[1]), values.dtype)
    joined = jnp.concatenate([previous, values, padding], axis=0)
    return lax.dynamic_update_slice_in_dim(joined, following, live_rows + half_span, 0)


def routing(destinations, data_index, blocks_out):
    plan_table = destinations[:, 0, :]
    mine_row = lax.dynamic_index_in_dim(plan_table, data_index, 0, keepdims=False)
    peers = plan_table.shape[0]
    slot_count = plan_table.shape[1]
    labels = jnp.arange(peers, dtype=jnp.int32)
    send_match = mine_row[:, None] == labels[None, :]
    positions = jnp.arange(slot_count, dtype=jnp.int32)
    send_block = jnp.sum(jnp.where(send_match, positions[:, None], 0), axis=0)
    send_live = jnp.any(send_match, axis=0)
    arrives = jnp.any(plan_table == data_index, axis=1)
    arrival_rank = jnp.cumsum(arrives.astype(jnp.int32)) - 1
    wanted = jnp.arange(blocks_out, dtype=jnp.int32)
    chosen = arrives[None, :] & (arrival_rank[None, :] == wanted[:, None])
    source_pick = jnp.sum(jnp.where(chosen, labels[None, :], 0), axis=1)
    return (mine_row, send_block, send_live, arrives, jnp.maximum(arrival_rank, 0), source_pick)


def select_blocks(blocks, block_index, keep_mask):
    picked = jnp.take(blocks, block_index, axis=0)
    return jnp.where(keep_mask[:, None, None], picked, jnp.zeros_like(picked))


def shards(frames, bounds, destinations, kernel, norm_gain, norm_shift, panel, cotangent):
    half_span = kernel.shape[0] // 2
    slot_rows = frames.shape[0]
    frame_features = frames.shape[1]
    slot_count = slot_rows // BLOCK_FRAMES
    blocks_out = cotangent.shape[0] // BLOCK_FRAMES
    total_live = float(cotangent.shape[0] * lax.axis_size("dp") * lax.axis_size("fsdp"))
    before_rows = bounds[0]
    after_rows = bounds[1]
    live_mask = (before_rows >= 0)[:, None]
    live_rows = jnp.sum((before_rows >= 0).astype(jnp.int32))
    padded = with_halo(rim_rows(frames, live_rows, half_span), ((("dp", "fsdp"), 0),), half_span)
    extended = extend(frames, padded[:half_span], padded[3 * half_span :], live_rows)
    filtered = conv_rows(extended, kernel, before_rows, after_rows)
    average = lax.psum(jnp.sum(filtered, axis=0), ("dp", "fsdp")) / total_live
    centred = jnp.where(live_mask, filtered - average, 0.0)
    variance = lax.psum(jnp.sum(centred * centred, axis=0), ("dp", "fsdp")) / total_live
    inverse = lax.rsqrt(variance + epsilon)
    whitened = (filtered - average) * inverse
    normed = whitened * norm_gain + norm_shift
    logistic = jax.nn.sigmoid(normed)
    layer_activation = jnp.where(live_mask, normed * logistic, 0.0).astype(jnp.bfloat16)
    mine_row, send_block, send_live, arrives, arrival_rank, source_pick = routing(
        destinations, lax.axis_index("dp"), blocks_out
    )
    outgoing = select_blocks(
        layer_activation.reshape(slot_count, BLOCK_FRAMES, frame_features), send_block, send_live
    )
    incoming = lax.all_to_all(outgoing, "dp", split_axis=0, concat_axis=0, tiled=True)
    left_rows = jnp.take(incoming, source_pick, axis=0).reshape(
        blocks_out * BLOCK_FRAMES, frame_features
    )
    columns = left_rows
    forward_sum = jnp.dot(
        columns,
        lax.all_gather(panel, "fsdp", axis=0, tiled=True),
        preferred_element_type=jnp.float32,
    )
    backward_sum = lax.dot_general(
        cotangent,
        lax.all_gather(panel, "fsdp", axis=0, tiled=True),
        (((1,), (1,)), ((), ())),
        preferred_element_type=jnp.float32,
    )
    projected = forward_sum.astype(jnp.bfloat16)
    back_act = backward_sum.astype(jnp.bfloat16)
    sent_back = select_blocks(
        back_act.reshape(blocks_out, BLOCK_FRAMES, frame_features), arrival_rank, arrives
    )
    came_back = lax.all_to_all(sent_back, "dp", split_axis=0, concat_axis=0, tiled=True)
    act_grad = select_blocks(came_back, jnp.maximum(mine_row, 0), mine_row >= 0).reshape(
        slot_rows, frame_features
    )
    columns = left_rows
    partial_grad = lax.psum_scatter(
        lax.dot_general(
            columns, cotangent, (((0,), (0,)), ((), ())), preferred_element_type=jnp.float32
        ),
        "fsdp",
        scatter_dimension=0,
        tiled=True,
    )
    panel_grad = lax.psum(partial_grad, "dp")
    normed_grad = act_grad.astype(jnp.float32) * (logistic + normed * logistic * (1.0 - logistic))
    gain_grad, shift_grad = lax.psum(
        (jnp.sum(normed_grad * whitened, axis=0), jnp.sum(normed_grad, axis=0)), ("dp", "fsdp")
    )
    inner = normed_grad - shift_grad / total_live - whitened * gain_grad / total_live
    conv_grad = jnp.where(live_mask, norm_gain * inverse * inner, 0.0)
    kernel_grad = lax.psum(
        kernel_terms(extended, conv_grad, before_rows, after_rows, kernel.shape[0]), ("dp", "fsdp")
    )
    grad_padded = with_halo(
        rim_rows(conv_grad, live_rows, half_span).astype(jnp.bfloat16),
        ((("dp", "fsdp"), 0),),
        half_span,
    ).astype(jnp.float32)
    grad_extended = extend(
        conv_grad, grad_padded[:half_span], grad_padded[3 * half_span :], live_rows
    )
    input_grad = conv_back(grad_extended, kernel, before_rows, after_rows).astype(jnp.bfloat16)
    return (projected, input_grad, panel_grad, kernel_grad, jnp.stack([gain_grad, shift_grad]))


def solution(mesh):
    placed = (
        P(("dp", "fsdp"), None),
        P(None, ("dp", "fsdp")),
        P(None, "fsdp", None),
        P(),
        P(),
        P(),
        P("fsdp", None),
        P(("dp", "fsdp"), None),
    )
    return jax.shard_map(
        shards,
        mesh=mesh,
        in_specs=placed,
        out_specs=(P(("dp", "fsdp"), None), P(("dp", "fsdp"), None), P("fsdp", None), P(), P()),
        check_vma=False,
    )
```

profile of v0, /device:TPU:1, one launch (start us, length us, event | category | flops | bytes accessed | tf_op | source)
XLA Modules:
  0.0 1045.4 jit_solution(7323071969999638511)
XLA Ops:
  7.2 0.0 all-gather.2.cloned.1.call-start
  7.2 0.7 all-gather.2.cloned.1.call-update
  7.9 0.8 compare_reduce_fusion.9
  8.7 0.6 convert_reduce_fusion
  10.7 0.8 fusion.64
  11.5 4.4 collective-permute-start
  15.9 5.0 collective-permute-start.1
  20.9 1.1 compare_reduce_fusion
  22.0 0.1 copy.15
  22.1 0.7 broadcast_compare_fusion.1
  22.8 0.1 maximum_reduce_fusion
  22.9 0.1 select_reduce_fusion
  23.0 0.1 fusion.55
  23.2 1.3 fusion.65
  25.8 0.1 pad.11.clone
  25.9 3.7 maximum_maximum_fusion.1
  29.6 1.4 dynamic_update_slice.6
  31.0 150.3 %all-gather.2.cloned.1.call-done = bf16[2048,2048]{1,0:T(8,128)(2,1)} async-done(((bf16[256,2048]{1,0:T(8,128)(2,1)}), bf16[2048,2048]{1,0:T(8,128)(2,1)}) %all-gather.2.cloned.1.call-update) | async-done | bytes 8388624 | tf_op jit(solution)/shard_map/all_gather | solution.py:137
  181.3 6.8 convolution_convert_fusion
  188.1 2.0 gather_fusion.1
  190.1 3.2 select_select_fusion.2
  193.3 7.3 all-to-all-start.1
  200.6 19.5 %fusion.62 = (f32[2048]{0:T(1024)S(1)}, f32[512,2048]{1,0:T(8,128)}) fusion(f32[2048]{0:T(1024)S(1)} %bitcast.65, bf16[520,2048]{1,0:T(8,128)(2,1)} %dynamic_update_slice.6, pred[512]{0:T(512)(128)(4,1)S(1)} %get-tuple-element.56, f32[2048]{0:T(1024)S(1)} %bitcast.67, pred[512]{0:T(512)(128)(4,1)S(1)} %get-tuple-element.57, f32[2048]{0:T(1024)S(1)} %bitcast.53, ...), kind=kLoop, calls=%fused_computation.152 | loop fusion | flops 37746688 | bytes 23155200 | tf_op jit(solution)/shard_map/reduce_sum | solution.py:116
  220.1 67.7 %psum.42 = f32[2048]{0:T(1024)S(1)} all-reduce(f32[2048]{0:T(1024)S(1)} %get-tuple-element.34), channel_id=1, replica_groups=mesh['dp'=16,'fsdp'=8] {'dp','fsdp'}, use_global_device_ids=true, to_apply=%region_6.7 | all-reduce | flops 2048 | bytes 16384 | tf_op jit(solution)/shard_map/psum | solution.py:116
  287.9 2.8 multiply_reduce_fusion.1
  290.7 62.8 %psum.43 = f32[2048]{0:T(1024)S(1)} all-reduce(f32[2048]{0:T(1024)S(1)} %multiply_reduce_fusion.1), channel_id=1, replica_groups=mesh['dp'=16,'fsdp'=8] {'dp','fsdp'}, use_global_device_ids=true, to_apply=%region_8.9 | all-reduce | flops 2048 | bytes 16384 | tf_op jit(solution)/shard_map/psum | solution.py:118
  353.5 3.6 gather_fusion.3
  357.1 2.0 select_select_fusion
  359.1 0.7 copy-done.2
  359.9 4.1 fusion.60
  364.0 3.6 gather_fusion.2
  367.6 3.2 select_select_fusion.1
  370.8 5.3 all-to-all-start
  376.1 0.0 reduce-scatter.2.cloned.1.call-start
  376.2 0.1 select_reduce_fusion.1
  376.3 0.1 broadcast_in_dim.277
  376.4 0.1 broadcast_in_dim.278
  376.5 28.2 %all-to-all-done = bf16[16,32,2048]{2,1,0:T(8,128)(2,1)} async-done(((bf16[16,32,2048]{2,1,0:T(8,128)(2,1)}), bf16[16,32,2048]{2,1,0:T(8,128)(2,1)}, u32[]{:S(2)}, u32[]{:S(2)}) %all-to-all-start) | async-done | bytes 2097184 | tf_op jit(solution)/shard_map/all_to_all | solution.py:130
  404.7 3.4 gather_fusion
  408.1 1.6 bitcast_select_fusion
  409.7 8.1 fusion.67
  417.8 0.0 reduce-scatter.2.cloned.1.call-update
  417.8 0.0 all-reduce.6.cloned.1.call-start
  417.9 0.1 pad.4.clone
  418.0 98.3 %all-reduce = (f32[2048]{0:T(1024)S(1)}, f32[2048]{0:T(1024)S(1)}) all-reduce(f32[2048]{0:T(1024)S(1)} %get-tuple-element.16, f32[2048]{0:T(1024)S(1)} %get-tuple-element.15), channel_id=1, replica_groups=mesh['dp'=16,'fsdp'=8] {'dp','fsdp'}, use_global_device_ids=true, to_apply=%region_13.15 | all-reduce | flops 4096 | bytes 32768 | tf_op jit(solution)/shard_map/psum | solution.py:166
  516.3 18.1 %fusion.34 = (f32[2048]{0:T(1024)S(1)}, f32[2048]{0:T(1024)S(1)}, f32[2048]{0:T(1024)S(1)}, f32[2048]{0:T(1024)S(1)}, f32[2048]{0:T(1024)S(1)}, /*index=5*/f32[2...) fusion(pred[512]{0:T(512)(128)(4,1)S(1)} %get-tuple-element.56, ...), kind=kLoop, calls=%fused_computation.57 | loop fusion | flops 57653248 | bytes 29496320 | tf_op jit(solution)/shard_map/reduce_sum | solution.py:62
  534.4 1.9 copy-done.4
  536.3 3.7 collective-permute-start.3
  540.0 1.9 collective-permute-start.2
  541.9 1.4 stack.46
  543.3 0.0 all-reduce.6.cloned.1.call-update
  543.3 0.3 all-reduce.4.cloned.1.call-start
  543.6 0.6 pad_maximum_fusion.3
  544.2 3.0 collective-permute-done.2
  547.3 4.7 maximum_maximum_fusion
  552.0 1.5 dynamic_update_slice.7
  553.5 191.2 %reduce-scatter.2.cloned.1.call-done = f32[256,2048]{1,0:T(8,128)} async-done(((f32[2048,2048]{1,0:T(8,128)}), f32[256,2048]{1,0:T(8,128)}) %reduce-scatter.2.cloned.1.call-update) | async-done | bytes 2097168 | tf_op jit(solution)/shard_map/reduce_scatter | solution.py:156
  744.7 0.0 all-reduce.4.cloned.1.call-update
  744.7 23.0 %fusion.37 = bf16[512,2048]{1,0:T(8,128)(2,1)} fusion(f32[520,2048]{1,0:T(8,128)} %dynamic_update_slice.7, f32[2048]{0:T(1024)S(1)} %bitcast.66, f32[2048]{0:T(1024)S(1)} %bitcast.68, f32[2048]{0:T(1024)S(1)} %bitcast.54, f32[2048]{0:T(1024)S(1)} %bitcast.56, f32[2048]{0:T(1024)S(1)} %bitcast.58, f32[2048]{0:T(1024)S(1)} %bitcast.60, f32[2048]{0:T(1024)S(1)} %bitcast.62, ...), kind=kLoop, calls=%fused_computation.61 | loop fusion | flops 28311552 | bytes 39924224 | tf_op jit(solution)/shard_map/convert_element_type | solution.py:182
  767.8 8.0 convolution_convert_fusion.1
  775.8 115.3 %all-reduce.6.cloned.1.call-done = f32[9,2048]{1,0:T(8,128)} async-done(((f32[9,2048]{1,0:T(8,128)}), f32[9,2048]{1,0:T(8,128)}) %all-reduce.6.cloned.1.call-update) | async-done | bytes 73744 | tf_op jit(solution)/shard_map/psum | solution.py:171
  891.1 143.9 %all-reduce.4.cloned.1.call-done = f32[256,2048]{1,0:T(8,128)} async-done(((f32[256,2048]{1,0:T(8,128)}), f32[256,2048]{1,0:T(8,128)}) %all-reduce.4.cloned.1.call-update) | async-done | bytes 2097168 | tf_op jit(solution)/shard_map/psum | solution.py:164
  1035.0 3.1 copy.20
  1038.2 0.7 copy.21
  (38 shorter events, 0.2 us)
Async XLA Ops:
  7.2 174.1 %copy-start = (bf16[384,2048]{1,0:T(8,128)(2,1)S(1)}, bf16[384,2048]{1,0:T(8,128)(2,1)}, u32[]{:S(2)}) copy-start(bf16[384,2048]{1,0:T(8,128)(2,1)} %param.17) | copy-start | bytes 4718596
  7.2 174.1 %all-gather.2.cloned.1.call-start = ((), (), s32[]{:S(2)}) async-start(), calls=%async_computation.3 | async-start | bytes 9437184 | tf_op jit(solution)/shard_map/all_gather | solution.py:137
  11.5 14.4 %collective-permute-start = (bf16[4,2048]{1,0:T(4,128)(2,1)S(1)}, bf16[4,2048]{1,0:T(4,128)(2,1)S(1)}, u32[]{:S(2)}, u32[]{:S(2)}) collective-permute-start(bf16[4,2048]{1,0:T(4,128)(2,1)S(1)} %get-tuple-element.40), channel_id=1, source_target_pairs={{0,1},{1,2},{2,3},{3,4},{4,5},{5,6},{6,7},{7,8},{8,9},{9,10},{10,1... | collective-permute-start | bytes 49160 | tf_op jit(solution)/shard_map/ppermute | solution.py:17
  15.9 13.7 %collective-permute-start.1 = (bf16[4,2048]{1,0:T(4,128)(2,1)S(1)}, bf16[4,2048]{1,0:T(4,128)(2,1)S(1)}, u32[]{:S(2)}, u32[]{:S(2)}) collective-permute-start(bf16[4,2048]{1,0:T(4,128)(2,1)S(1)} %get-tuple-element.39), channel_id=1, source_target_pairs={{1,0},{2,1},{3,2},{4,3},{5,4},{6,5},{7,6},{8,7},{9,8},{10,9},{11,1... | collective-permute-start | bytes 49160 | tf_op jit(solution)/shard_map/ppermute | solution.py:20
  193.3 160.2 %all-to-all-start.1 = ((bf16[16,32,2048]{2,1,0:T(8,128)(2,1)}), bf16[16,32,2048]{2,1,0:T(8,128)(2,1)}, u32[]{:S(2)}, u32[]{:S(2)}) async-start(bf16[16,32,2048]{2,1,0:T(8,128)(2,1)} %select_select_fusion.2), calls=%async_computation.1 | async-start | bytes 4194304 | tf_op jit(solution)/shard_map/all_to_all | solution.py:151
  220.1 133.3 %copy-start.6 = (f32[2048]{0:T(1024)S(1)}, f32[2048]{0:T(1024)}, u32[]{:S(2)}) copy-start(f32[2048]{0:T(1024)} %param.14) | copy-start | bytes 24580
  353.5 5.7 copy-start.7
  357.1 2.8 copy-start.2
  359.1 4.9 copy-start.3
  370.8 33.8 %all-to-all-start = ((bf16[16,32,2048]{2,1,0:T(8,128)(2,1)}), bf16[16,32,2048]{2,1,0:T(8,128)(2,1)}, u32[]{:S(2)}, u32[]{:S(2)}) async-start(bf16[16,32,2048]{2,1,0:T(8,128)(2,1)} %select_select_fusion.1), calls=%async_computation | async-start | bytes 4194304 | tf_op jit(solution)/shard_map/all_to_all | solution.py:130
  376.1 368.6 %reduce-scatter.2.cloned.1.call-start = ((), (), s32[]{:S(2)}) async-start(), calls=%async_computation.4 | async-start | bytes 18874368 | tf_op jit(solution)/shard_map/reduce_scatter | solution.py:156
  417.8 473.3 %all-reduce.6.cloned.1.call-start = ((), (), s32[]{:S(2)}) async-start(), calls=%async_computation.6 | async-start | bytes 262144 | tf_op jit(solution)/shard_map/psum | solution.py:171
  534.4 1.9 copy-start.4
  536.3 7.9 collective-permute-start.3
  540.0 7.3 collective-permute-start.2
  543.3 491.7 %all-reduce.4.cloned.1.call-start = ((), (), s32[]{:S(2)}) async-start(), calls=%async_computation.5 | async-start | bytes 4194304 | tf_op jit(solution)/shard_map/psum | solution.py:164
  767.8 271.1 %copy-start.1 = (bf16[384,2048]{1,0:T(8,128)(2,1)S(1)}, bf16[384,2048]{1,0:T(8,128)(2,1)}, u32[]{:S(2)}) copy-start(bf16[384,2048]{1,0:T(8,128)(2,1)} %param.17) | copy-start | bytes 4718596
  891.1 147.1 %copy-start.5 = (f32[9,2048]{1,0:T(8,128)S(1)}, f32[9,2048]{1,0:T(8,128)}, u32[]{:S(2)}) copy-start(f32[9,2048]{1,0:T(8,128)} %all-reduce.6.cloned.1.call-done) | copy-start | bytes 221188
Sparse Core Ops, SparseCore 0:
  9.7 171.5 all-gather.1
  418.0 326.6 reduce-scatter.1
  750.0 141.0 all-reduce.5
  893.6 141.3 all-reduce.3
where the time goes:
time: 1050 us
  waiting for transfers between devices  633 us (60%)
  blocking collectives  229 us (22%)
  other arithmetic  90.5 us (9%)
  starting transfers between devices  28 us (3%)
  local copies, waits for them, and re-layouts  25.9 us (2%)
  matrix products  22.9 us (2%)
  between operations  16.6 us (2%)
    reduce_scatter x1, waiting for transfers between devices, shards(): lax.psum_scatter(lax.dot_general(columns, cotangent, (((0,), (0,)), ((),...  191 us
    all_gather x1, waiting for transfers between devices, shards(): lax.all_gather(panel, 'fsdp', axis=0, tiled=True)  150 us
    psum x1, waiting for transfers between devices, shards(): panel_grad = lax.psum(partial_grad, 'dp')  144 us
    psum x1, waiting for transfers between devices, shards(): lax.psum(kernel_terms(extended, conv_grad, before_rows, after_rows, kerne...  115 us
    psum x1, blocking collectives, shards(): lax.psum((jnp.sum(normed_grad * whitened, axis=0), jnp.sum(normed_grad, a...  98.3 us
    psum x1, blocking collectives, shards(): average = lax.psum(jnp.sum(filtered, axis=0), ('dp', 'fsdp')) / total_live  67.7 us
    psum x1, blocking collectives, shards(): lax.psum(jnp.sum(centred * centred, axis=0), ('dp', 'fsdp')) / total_live  62.8 us
    all_to_all x1, waiting for transfers between devices, shards(): lax.all_to_all(outgoing, 'dp', split_axis=0, concat_axis=0, tiled=True)  28.2 us
  transfers between devices with their start and end apart: 10, of which 6 were waited for; matrix products, arithmetic and copies ran while one was open for 9% of the time, Pallas kernels for 0%

commit v1 on v0

v1 whole, which is shorter than its diff:
```python
import jax
import jax.numpy as jnp
from jax import lax
from jax.experimental import pallas as pl
from jax.experimental.pallas import tpu as pltpu
from jax.sharding import PartitionSpec as P

MESH = pl.DeviceIdType.MESH
F32 = jnp.float32
BF16 = jnp.bfloat16
EPSILON = 1e-05

D = 2048
TAPS = 9
BLOCK = 32
SLOTS = 512
ROWS = 384
N_DP = 16
N_FSDP = 8
CHUNKS = D // 128
TOTAL = float(ROWS * N_DP * N_FSDP)

RANK, DEST, SEND, PICK, LIVE = 0, 16, 32, 48, 60


def routing(destinations, data_index):
    plan_table = destinations[:, 0, :]
    mine_row = lax.dynamic_index_in_dim(plan_table, data_index, 0, keepdims=False)
    labels = jnp.arange(N_DP, dtype=jnp.int32)
    peers = (data_index + labels) % N_DP
    send_match = mine_row[None, :] == peers[:, None]
    send_row = jnp.sum(jnp.where(send_match, labels[None, :], 0), axis=1)
    arrives = jnp.any(plan_table == data_index, axis=1)
    earlier = (labels[None, :] < peers[:, None]) & arrives[None, :]
    rank_row = jnp.minimum(jnp.sum(earlier.astype(jnp.int32), axis=1), 11)
    source_rank = jnp.sum(((labels[None, :] < labels[:, None]) & arrives[None, :]).astype(jnp.int32), axis=1)
    wanted = jnp.arange(12, dtype=jnp.int32)
    chosen = arrives[None, :] & (source_rank[None, :] == wanted[:, None])
    source_slot = (data_index - labels + N_DP) % N_DP
    pick_slot = jnp.sum(jnp.where(chosen, source_slot[None, :], 0), axis=1)
    back_slot = jnp.where(mine_row >= 0, (data_index - mine_row + N_DP) % N_DP, 0)
    blocks = jnp.sum((mine_row >= 0).astype(jnp.int32))
    tail = jnp.stack([BLOCK * blocks, 2 * blocks - 1, BLOCK * blocks - 8, blocks])
    idx = jnp.concatenate(
        [rank_row, back_slot, send_row, pick_slot, tail]
    )
    flags = jnp.concatenate([labels < blocks, labels + 1 == blocks]).astype(F32)
    count = jnp.full((8, 128), (BLOCK * blocks).astype(F32))
    return idx, jnp.concatenate([jnp.broadcast_to(flags[:, None], (32, 128)), count])


class Sems:
    def __init__(self):
        self.used = 0

    def take(self, count):
        at = self.used
        self.used += count
        return at


SEMS = Sems()
S_HALO = SEMS.take(2)
S_OWN = SEMS.take(3)
S_FWD = SEMS.take(2)
S_FAR = SEMS.take(4)
S_PAIR = SEMS.take(7)
S_COT = SEMS.take(16)
S_ST1 = SEMS.take(8)
S_ST2 = SEMS.take(16)
S_ACT = SEMS.take(16)
S_AT = SEMS.take(1)
S_CP = SEMS.take(1)
S_NG1 = SEMS.take(8)
S_NG2 = SEMS.take(16)
S_BHALO = SEMS.take(4)
S_R1 = SEMS.take(4)
S_R2 = SEMS.take(4)
S_R3 = SEMS.take(4)
S_GAT = SEMS.take(8)
S_GPAIR = SEMS.take(1)
S_K1 = SEMS.take(16)
S_K2 = SEMS.take(8)
S_K3 = SEMS.take(16)


def fused(
    idx,
    flags,
    bounds,
    frames,
    cotangent,
    panel,
    kern,
    gain,
    shift,
    mapped,
    igrad,
    pgrad,
    kgrad,
    ngrad,
    fr,
    cot,
    cs,
    cr,
    cp,
    cpp,
    ext,
    filt,
    ngx,
    msk,
    pan,
    act,
    ar,
    at,
    atp,
    gp,
    r1,
    s1,
    r2,
    s2,
    r3,
    pgb,
    pst,
    mst,
    htrail,
    hprev,
    hnext,
    st1,
    st2,
    stat,
    ng1,
    ng2,
    bsend,
    brecv,
    kg,
    kg1,
    kg2,
    kg3,
    ssem,
    rsem,
    lsem,
):
    dp = lax.axis_index("dp")
    f = lax.axis_index("fsdp")
    c = dp % 2
    zh = (dp // 2) % 2
    x = dp // 4
    y = f // 2
    zl = f % 2
    z = zh * 2 + zl
    partner = dp + 1 - 2 * c
    me = dp * N_FSDP + f
    follow = (me + 1) % (N_DP * N_FSDP)
    lead = (me + N_DP * N_FSDP - 1) % (N_DP * N_FSDP)

    def remote(src, dst, sem, to_dp, to_f):
        return pltpu.make_async_remote_copy(
            src_ref=src,
            dst_ref=dst,
            send_sem=ssem.at[sem],
            recv_sem=rsem.at[sem],
            device_id=(to_dp, to_f),
            device_id_type=MESH,
        )

    def loop(count, body, start=0):
        def step(k, carry):
            body(k)
            return carry

        lax.fori_loop(start, count, step, 0)

    def lanes(j):
        return pl.ds(pl.multiple_of(j * 128, 128), 128)

    def rows(at_row, count):
        return pl.ds(pl.multiple_of(at_row, count), count)

    load_frames = pltpu.make_async_copy(frames, fr, lsem.at[0])
    load_cot = pltpu.make_async_copy(cotangent, cot, lsem.at[1])
    load_panel = pltpu.make_async_copy(panel, pan.at[rows(f * 256, 256)], lsem.at[2])
    load_frames.start()
    load_panel.start()
    load_cot.start()

    barrier = pltpu.get_barrier_semaphore()

    def greet(to_dp, to_f):
        pl.semaphore_signal(barrier, inc=1, device_id=(to_dp, to_f), device_id_type=MESH)

    loop(N_DP, lambda k: greet((dp + k) % N_DP, f), 1)
    loop(N_FSDP, lambda k: greet(dp, (f + k) % N_FSDP), 1)
    greet(follow // N_FSDP, follow % N_FSDP)
    greet(lead // N_FSDP, lead % N_FSDP)
    greet(x * 4 + (1 - zh) * 2 + c, y * 2 + 1 - zl)

    for q in range(4):
        part = slice(128 * q, 128 * q + 128)
        before = jnp.broadcast_to(bounds[0:1, part].astype(F32), (128, 128)).T
        after = jnp.broadcast_to(bounds[1:2, part].astype(F32), (128, 128)).T
        for tap in range(TAPS):
            o = tap - 4
            keep = (before >= float(max(-o, 0))) & (after >= float(max(o, 0)))
            msk[tap, part, :] = jnp.where(keep, 1.0, 0.0)

    pl.semaphore_wait(barrier, 25)

    def unit(f_of):
        return pan.at[pl.ds(pl.multiple_of(f_of * 256 + c * 128, 128), 128)]

    def half_unit(f_of, h):
        return pan.at[pl.ds(pl.multiple_of(f_of * 256 + c * 128 + h * 64, 64), 64)]

    def shard_at(dy, dz):
        return ((y + dy) % 4) * 2 + (zl + dz) % 2

    f_z, f_up, f_down = shard_at(0, 1), shard_at(1, 0), shard_at(3, 0)
    f_upz, f_downz = shard_at(1, 1), shard_at(3, 1)
    f_far, f_farz = shard_at(2, 0), shard_at(2, 1)

    def send_unit(f_of, sem, to_f):
        return remote(unit(f_of), unit(f_of), sem, dp, to_f)

    def send_half(f_of, h, sem, to_f):
        return remote(half_unit(f_of, h), half_unit(f_of, h), sem, dp, to_f)

    def to_partner(f_of, n):
        return remote(unit(f_of), unit(f_of), S_PAIR + n, partner, f)

    own_copies = [
        send_unit(f, S_OWN, f_z),
        send_unit(f, S_OWN + 1, f_up),
        send_unit(f, S_OWN + 2, f_down),
    ]
    fwd_copies = [send_unit(f_z, S_FWD, f_up), send_unit(f_z, S_FWD + 1, f_down)]
    far_copies = [
        send_half(f_down, 0, S_FAR, f_up),
        send_half(f_up, 1, S_FAR + 1, f_down),
        send_half(f_downz, 0, S_FAR + 2, f_up),
        send_half(f_upz, 1, S_FAR + 3, f_down),
    ]
    pair_copies = [
        to_partner(g, n)
        for n, g in enumerate([f_z, f_down, f_up, f_downz, f_upz, f_far, f_farz])
    ]

    load_frames.wait()
    htrail[...] = fr[idx[LIVE + 1]]
    halo_next = remote(htrail, hprev, S_HALO, follow // N_FSDP, follow % N_FSDP)
    halo_prev = remote(fr.at[0], hnext, S_HALO + 1, lead // N_FSDP, lead % N_FSDP)
    halo_next.start()
    halo_prev.start()

    load_panel.wait()
    for copy in own_copies:
        copy.start()

    load_cot.wait()

    def cot_block(k):
        return cot[idx[RANK + k]]

    cr[0] = cot_block(0)

    def cot_copy(k):
        return remote(cs.at[k], cr.at[k], S_COT + k, (dp + k) % N_DP, f)

    def send_cot(k):
        cs[k] = cot_block(k)
        cot_copy(k).start()

    loop(N_DP, send_cot, 1)

    def widen(j):
        for q in range(4):
            part = fr[8 * q : 8 * q + 8, :, lanes(j)].reshape(128, 128)
            ext[j, 8 + 128 * q : 136 + 128 * q, :] = part.astype(F32)
        ext[j, 520:528, :] = jnp.zeros((8, 128), F32)

    loop(CHUNKS, widen)

    halo_next.wait_recv()
    halo_prev.wait_recv()

    def place(ref, j, previous, following):
        ref[j, 0:8, :] = previous
        for b in range(8, 17):
            at_row = 8 + BLOCK * b
            here = ref[j, at_row : at_row + 8, :]
            last = flags[15 + b : 16 + b, :]
            ref[j, at_row : at_row + 8, :] = here * (1.0 - last) + following * last

    def place_frames(j):
        place(
            ext,
            j,
            hprev[:, lanes(j)].astype(F32)[8:16],
            hnext[:, lanes(j)].astype(F32)[0:8],
        )

    loop(CHUNKS, place_frames)

    def fold(value):
        return jnp.sum(value, axis=0, keepdims=True)

    def conv(j):
        taps = kern[:, lanes(j)]

        def part(i, total):
            base = i * 64
            accum = jnp.zeros((64, 128), F32)
            for tap in range(TAPS):
                window = ext[j, pl.ds(base + 4 + tap, 64), :] * taps[tap : tap + 1]
                accum = accum + msk[tap, rows(base, 64), :] * window
            filt[j, rows(base, 64), :] = accum
            return total + jnp.sum(accum.reshape(8, 8, 128), axis=0)

        total = lax.fori_loop(0, 8, part, jnp.zeros((8, 128), F32))
        total = fold(total)
        mean = total / flags[32:33, :]

        def spread(i, total):
            base = i * 64
            off = (filt[j, rows(base, 64), :] - mean) * msk[4, rows(base, 64), :]
            return total + jnp.sum((off * off).reshape(8, 8, 128), axis=0)

        squares = fold(lax.fori_loop(0, 8, spread, jnp.zeros((8, 128), F32)))
        st1[0, pl.ds(j, 1), :] = total
        st1[0, pl.ds(16 + j, 1), :] = squares

    loop(CHUNKS, conv)
    st1[0, 32:40, :] = flags[32:40, :]

    def over_fsdp(buf, sem):
        def copy(k):
            return remote(buf.at[0], buf.at[k], sem + k, dp, (f + k) % N_FSDP)

        return copy

    def over_dp(buf, sem):
        def copy(k):
            return remote(buf.at[0], buf.at[k], sem + k, (dp + k) % N_DP, f)

        return copy

    def begin(copy, count):
        loop(count, lambda k: copy(k).start(), 1)

    def arrive(copy, count):
        loop(count, lambda k: copy(k).wait_recv(), 1)

    def merge(buf, count, mine):
        def slot(p):
            return (mine - p + count) % count

        def add(p, carry):
            sums, number = carry
            return sums + buf[slot(p), 0:16, :], number + buf[slot(p), 32:40, :]

        sums, number = lax.fori_loop(
            0, count, add, (jnp.zeros((16, 128), F32), jnp.zeros((8, 128), F32))
        )
        mean = sums / jnp.concatenate([number, number], axis=0)

        def spread(p, squares):
            n_p = buf[slot(p), 32:40, :]
            n_p = jnp.concatenate([n_p, n_p], axis=0)
            off = buf[slot(p), 0:16, :] / n_p - mean
            return squares + (buf[slot(p), 16:32, :] + n_p * off * off)

        squares = lax.fori_loop(0, count, spread, jnp.zeros((16, 128), F32))
        return sums, squares, number

    def ordered(buf, count, mine, shape):
        def add(p, total):
            return total + buf[(mine - p + count) % count]

        return lax.fori_loop(0, count, add, jnp.zeros(shape, F32))

    copy_st1 = over_fsdp(st1, S_ST1)
    copy_st2 = over_dp(st2, S_ST2)
    begin(copy_st1, N_FSDP)

    own_copies[0].wait_recv()
    fwd_copies[0].start()
    fwd_copies[1].start()
    pair_copies[0].start()
    own_copies[1].wait_recv()
    far_copies[0].start()
    pair_copies[1].start()
    own_copies[2].wait_recv()
    far_copies[1].start()
    pair_copies[2].start()

    arrive(copy_st1, N_FSDP)
    sums, squares, number = merge(st1, N_FSDP, f)
    st2[0, 0:16, :] = sums
    st2[0, 16:32, :] = squares
    st2[0, 32:40, :] = number
    begin(copy_st2, N_DP)

    fwd_copies[0].wait_recv()
    far_copies[2].start()
    pair_copies[3].start()
    fwd_copies[1].wait_recv()
    far_copies[3].start()
    pair_copies[4].start()

    loop(N_DP, lambda k: cot_copy(k).wait_recv(), 1)

    def back_block(b):
        block = cr[idx[DEST + b]]
        kept = jnp.broadcast_to(flags[pl.ds(b, 1), 0:1].astype(BF16), (BLOCK, D))
        cp[rows(b * BLOCK, BLOCK), :] = block * kept

    loop(16, back_block)
    copy_cp = remote(cp, cpp, S_CP, partner, f)
    copy_cp.start()

    arrive(copy_st2, N_DP)
    sums, squares, number = merge(st2, N_DP, dp)
    stat[0:16, :] = sums / TOTAL
    stat[16:32, :] = lax.rsqrt(squares / TOTAL + EPSILON)

    def act_grad(f_of):
        value = lax.dot_general(
            cp[...],
            pan[rows(f_of * 256, 256), :],
            (((1,), (1,)), ((), ())),
            preferred_element_type=F32,
        )
        value = value.astype(BF16).astype(F32)
        ngx[f_of * 2, 8:520, :] = value[:, 0:128]
        ngx[f_of * 2 + 1, 8:520, :] = value[:, 128:256]

    far_copies[0].wait_recv()
    far_copies[1].wait_recv()
    pair_copies[5].start()
    far_copies[2].wait_recv()
    far_copies[3].wait_recv()
    pair_copies[6].start()
    for copy in pair_copies:
        copy.wait_recv()
    loop(N_FSDP, act_grad)

    def activate(j):
        average = stat[pl.ds(j, 1), :]
        inverse = stat[pl.ds(16 + j, 1), :]
        g = gain[pl.ds(j, 1), :]
        b = shift[pl.ds(j, 1), :]
        sum_w = jnp.zeros((8, 128), F32)
        sum_1 = jnp.zeros((8, 128), F32)
        for q in range(4):
            base = 128 * q
            keep = msk[4, base : base + 128, :]
            whitened = (filt[j, base : base + 128, :] - average) * inverse
            normed = whitened * g + b
            logistic = 1.0 / (1.0 + jnp.exp(-normed))
            value = normed * logistic * keep
            slope = logistic + normed * logistic * (1.0 - logistic)
            grad = ngx[j, 8 + base : 136 + base, :] * slope
            filt[j, base : base + 128, :] = whitened
            ngx[j, 8 + base : 136 + base, :] = grad
            act[4 * q : 4 * q + 4, :, lanes(j)] = value.astype(BF16).reshape(4, BLOCK, 128)
            at[j % 2, rows((j // 2) * 128, 128), base : base + 128] = value.T.astype(BF16)
            sum_w = sum_w + jnp.sum((grad * whitened).reshape(16, 8, 128), axis=0)
            sum_1 = sum_1 + jnp.sum(grad.reshape(16, 8, 128), axis=0)
        ng1[0, pl.ds(j, 1), :] = fold(sum_w)
        ng1[0, pl.ds(16 + j, 1), :] = fold(sum_1)
        bsend[0, j] = ngx[j, 8:16, :]
        bsend[1, j] = filt[j, 0:8, :]
        bsend[2, j] = ngx[j, pl.ds(idx[LIVE], 8), :]
        bsend[3, j] = filt[j, pl.ds(idx[LIVE + 2], 8), :]

    loop(CHUNKS, activate)

    copy_ng1 = over_fsdp(ng1, S_NG1)
    copy_ng2 = over_dp(ng2, S_NG2)
    begin(copy_ng1, N_FSDP)
    halo_copies = [
        remote(bsend.at[0], brecv.at[0], S_BHALO, lead // N_FSDP, lead % N_FSDP),
        remote(bsend.at[1], brecv.at[1], S_BHALO + 1, lead // N_FSDP, lead % N_FSDP),
        remote(bsend.at[2], brecv.at[2], S_BHALO + 2, follow // N_FSDP, follow % N_FSDP),
        remote(bsend.at[3], brecv.at[3], S_BHALO + 3, follow // N_FSDP, follow % N_FSDP),
    ]
    for copy in halo_copies:
        copy.start()
    copy_at = remote(at.at[1 - c], atp, S_AT, partner, f)
    copy_at.start()

    def act_block(k):
        return act[idx[SEND + k]]

    ar[0] = act_block(0)

    def act_copy(k):
        return remote(cs.at[k], ar.at[k], S_ACT + k, (dp + k) % N_DP, f)

    def send_act(k):
        cot_copy(k).wait_send()
        cs[k] = act_block(k)
        act_copy(k).start()

    loop(N_DP, send_act, 1)

    arrive(copy_ng1, N_FSDP)
    ng2[0] = ordered(ng1, N_FSDP, f, (32, 128))
    begin(copy_ng2, N_DP)

    copy_cp.wait_recv()
    copy_at.wait_recv()
    first = y * (1 - c) + x * c
    second = x * (1 - c) + y * c

    def first_peer(a):
        return ((x * (1 - c) + a * c) * 4 + zh * 2 + c, (a * (1 - c) + y * c) * 2 + zl)

    def second_peer(b):
        return ((b * (1 - c) + x * c) * 4 + zh * 2 + c, (y * (1 - c) + b * c) * 2 + zl)

    def copy_r1(k):
        a = (first + k) % 4
        return remote(gp.at[a], r1.at[k - 1], S_R1 + k, *first_peer(a))

    def copy_r2(k):
        b = (second + k) % 4
        return remote(s1.at[b], r2.at[k - 1], S_R2 + k, *second_peer(b))

    def copy_r3(k):
        to_z = (z + k) % 4
        return remote(
            s2.at[to_z], r3.at[k - 1], S_R3 + k, x * 4 + (to_z // 2) * 2 + c, y * 2 + to_z % 2
        )

    for k in (1, 2, 3, 4):
        a = (first + k) % 4

        def product(b, a=a):
            y_of = a * (1 - c) + b * c
            x_of = b * (1 - c) + a * c
            d_rows = rows(y_of * 256, 256)
            columns = pl.ds(pl.multiple_of(x_of * 512, 512), 512)
            value = jnp.dot(at[c, d_rows, :], cp[:, columns], preferred_element_type=F32)
            value = value + jnp.dot(
                atp[d_rows, :], cpp[:, columns], preferred_element_type=F32
            )
            for h in range(2):
                for low in range(2):
                    piece = value[low * 128 : low * 128 + 128, h * 256 : h * 256 + 256]
                    gp[a, b, h * 2 + low] = piece.astype(BF16)

        loop(4, product)
        if k < 4:
            copy_r1(k).start()

    arrive(copy_ng2, N_DP)
    ng_total = ordered(ng2, N_DP, dp, (32, 128))
    stat[32:64, :] = ng_total
    for j in range(CHUNKS):
        ngrad[0:1, 128 * j : 128 * j + 128] = ng_total[j : j + 1]
        ngrad[1:2, 128 * j : 128 * j + 128] = ng_total[16 + j : 17 + j]
    for copy in halo_copies:
        copy.wait_recv()

    def back(j):
        taps = kern[:, lanes(j)]
        scale = gain[pl.ds(j, 1), :] * stat[pl.ds(16 + j, 1), :]
        mean_w = stat[pl.ds(32 + j, 1), :] / TOTAL
        mean_1 = stat[pl.ds(48 + j, 1), :] / TOTAL

        def center(grad, whitened):
            return scale * (grad - mean_1 - whitened * mean_w)

        for q in range(4):
            base = 128 * q
            ngx[j, 8 + base : 136 + base, :] = center(
                ngx[j, 8 + base : 136 + base, :], filt[j, base : base + 128, :]
            )
        ngx[j, 520:528, :] = jnp.zeros((8, 128), F32)
        place(
            ngx, j, center(brecv[2, j], brecv[3, j]), center(brecv[0, j], brecv[1, j])
        )

        def part(i, sums):
            base = i * 32
            accum = jnp.zeros((32, 128), F32)
            here = ext[j, pl.ds(pl.multiple_of(base + 8, 8), 32), :]
            new = []
            for tap in range(TAPS):
                window = ngx[j, pl.ds(base + 12 - tap, 32), :]
                window = window * msk[8 - tap, rows(base, 32), :]
                accum = accum + window * taps[tap : tap + 1]
                new.append(sums[tap] + jnp.sum((window * here).reshape(4, 8, 128), axis=0))
            fr[pl.ds(i * 2, 2), :, lanes(j)] = accum.astype(BF16).reshape(2, 16, 128)
            return tuple(new)

        sums = lax.fori_loop(
            0, 16, part, tuple(jnp.zeros((8, 128), F32) for _ in range(TAPS))
        )
        kg[j, 8:16, :] = jnp.zeros((8, 128), F32)
        for tap in range(TAPS):
            kg[j, tap : tap + 1, :] = fold(sums[tap])

    halo_prev.wait_send()
    loop(CHUNKS, back)
    store_igrad = pltpu.make_async_copy(fr, igrad, lsem.at[0])
    store_igrad.start()

    def copy_k1(k):
        peer = (dp + k) % N_DP
        return remote(kg.at[peer], kg1.at[k], S_K1 + k, peer, f)

    begin(copy_k1, N_DP)
    kg1[0] = kg[dp]

    for k in (1, 2, 3):
        copy_r1(k).wait_recv()

    def add_first(b):
        for n in range(4):
            value = gp[first, b, n].astype(F32)
            for k in range(3):
                value = value + r1[k, b, n].astype(F32)
            s1[b, n] = value.astype(BF16)

    loop(4, add_first)
    for k in (1, 2, 3):
        copy_r2(k).start()

    arrive(copy_k1, N_DP)
    kg2[0] = ordered(kg1, N_DP, dp, (16, 128))
    copy_k2 = over_fsdp(kg2, S_K2)
    begin(copy_k2, N_FSDP)

    loop(N_DP, lambda k: act_copy(k).wait_recv(), 1)

    def pick(r):
        cot[r] = ar[idx[PICK + r]]

    loop(12, pick)

    def project(n):
        columns = pl.ds(pl.multiple_of(n * 256, 256), 256)
        value = jnp.dot(cot[...].reshape(ROWS, D), pan[:, columns], preferred_element_type=F32)
        mst[:, columns] = value.astype(BF16)

    loop(4, project)

    for k in (1, 2, 3):
        copy_r2(k).wait_recv()

    def add_second(n):
        value = s1[second, n].astype(F32)
        for k in range(3):
            value = value + r2[k, n].astype(F32)
        s2[n] = value.astype(BF16)

    loop(4, add_second)
    for k in (1, 2, 3):
        copy_r3(k).start()

    arrive(copy_k2, N_FSDP)
    kg3[dp] = ordered(kg2, N_FSDP, f, (16, 128))

    def copy_k3(k):
        return remote(kg3.at[dp], kg3.at[dp], S_K3 + k, (dp + k) % N_DP, f)

    begin(copy_k3, N_DP)

    loop(8, project, 4)
    store_mapped = pltpu.make_async_copy(mst, mapped, lsem.at[1])
    store_mapped.start()

    for k in (1, 2, 3):
        copy_r3(k).wait_recv()
    value = s2[z].astype(F32)
    for k in range(3):
        value = value + r3[k].astype(F32)
    place_of = x * 2 + zh
    pgb[c, place_of] = value.astype(BF16)

    def copy_gather(k):
        to = (place_of + k) % 8
        mine = pgb.at[c, place_of]
        return remote(mine, mine, S_GAT + k, to * 2 + c, f)

    begin(copy_gather, 8)
    arrive(copy_gather, 8)
    copy_gpair = remote(pgb.at[c], pgb.at[c], S_GPAIR, partner, f)
    copy_gpair.start()

    arrive(copy_k3, N_DP)
    for j in range(CHUNKS):
        kgrad[:, 128 * j : 128 * j + 128] = kg3[j, 0:TAPS, :]

    copy_gpair.wait_recv()
    for u in range(8):
        pst[0:128, 256 * u : 256 * u + 256] = pgb[0, u].astype(F32)
        pst[128:256, 256 * u : 256 * u + 256] = pgb[1, u].astype(F32)
    store_pgrad = pltpu.make_async_copy(pst, pgrad, lsem.at[2])
    store_pgrad.start()

    halo_next.wait_send()
    for copy in own_copies + fwd_copies + far_copies + pair_copies + halo_copies:
        copy.wait_send()
    copy_cp.wait_send()
    copy_at.wait_send()
    copy_gpair.wait_send()
    for k in (1, 2, 3):
        copy_r1(k).wait_send()
        copy_r2(k).wait_send()
        copy_r3(k).wait_send()
    for copy in (copy_st2, act_copy, copy_ng2, copy_k1, copy_k3):
        loop(N_DP, lambda k, copy=copy: copy(k).wait_send(), 1)
    for copy in (copy_st1, copy_ng1, copy_k2, copy_gather):
        loop(N_FSDP, lambda k, copy=copy: copy(k).wait_send(), 1)
    store_igrad.wait()
    store_mapped.wait()
    store_pgrad.wait()


def shards(frames, bounds, destinations, kernel, norm_gain, norm_shift, panel, cotangent):
    idx, flags = routing(destinations, lax.axis_index("dp"))
    hbm = pl.BlockSpec(memory_space=pl.ANY)
    vmem = pl.BlockSpec(memory_space=pltpu.VMEM)
    shape = jax.ShapeDtypeStruct
    mapped, input_grad, *rest = pl.pallas_call(
        fused,
        out_shape=(
            shape((ROWS, D), BF16),
            shape((32, 16, D), BF16),
            shape((256, D), F32),
            shape((TAPS, D), F32),
            shape((2, D), F32),
        ),
        in_specs=[pl.BlockSpec(memory_space=pltpu.SMEM), vmem, vmem, hbm, hbm, hbm, vmem, vmem, vmem],
        out_specs=(hbm, hbm, hbm, vmem, vmem),
        scratch_shapes=[
            pltpu.VMEM((32, 16, D), BF16),
            pltpu.VMEM((12, BLOCK, D), BF16),
            pltpu.VMEM((16, BLOCK, D), BF16),
            pltpu.VMEM((16, BLOCK, D), BF16),
            pltpu.VMEM((SLOTS, D), BF16),
            pltpu.VMEM((SLOTS, D), BF16),
            pltpu.VMEM((CHUNKS, 528, 128), F32),
            pltpu.VMEM((CHUNKS, 512, 128), F32),
            pltpu.VMEM((CHUNKS, 528, 128), F32),
            pltpu.VMEM((TAPS, 512, 128), F32),
            pltpu.VMEM((D, D), BF16),
            pltpu.VMEM((16, BLOCK, D), BF16),
            pltpu.VMEM((16, BLOCK, D), BF16),
            pltpu.VMEM((2, 1024, 512), BF16),
            pltpu.VMEM((1024, 512), BF16),
            pltpu.VMEM((4, 4, 4, 128, 256), BF16),
            pltpu.VMEM((3, 4, 4, 128, 256), BF16),
            pltpu.VMEM((4, 4, 128, 256), BF16),
            pltpu.VMEM((3, 4, 128, 256), BF16),
            pltpu.VMEM((4, 128, 256), BF16),
            pltpu.VMEM((3, 128, 256), BF16),
            pltpu.VMEM((2, 8, 128, 256), BF16),
            pltpu.VMEM((256, D), F32),
            pltpu.VMEM((ROWS, D), BF16),
            pltpu.VMEM((16, D), BF16),
            pltpu.VMEM((16, D), BF16),
            pltpu.VMEM((16, D), BF16),
            pltpu.VMEM((N_FSDP, 40, 128), F32),
            pltpu.VMEM((N_DP, 40, 128), F32),
            pltpu.VMEM((64, 128), F32),
            pltpu.VMEM((N_FSDP, 32, 128), F32),
            pltpu.VMEM((N_DP, 32, 128), F32),
            pltpu.VMEM((4, CHUNKS, 8, 128), F32),
            pltpu.VMEM((4, CHUNKS, 8, 128), F32),
            pltpu.VMEM((CHUNKS, 16, 128), F32),
            pltpu.VMEM((N_DP, 16, 128), F32),
            pltpu.VMEM((N_FSDP, 16, 128), F32),
            pltpu.VMEM((CHUNKS, 16, 128), F32),
            pltpu.SemaphoreType.DMA((SEMS.used,)),
            pltpu.SemaphoreType.DMA((SEMS.used,)),
            pltpu.SemaphoreType.DMA((3,)),
        ],
        compiler_params=pltpu.CompilerParams(
            collective_id=0, has_side_effects=True, vmem_limit_bytes=62 * 1024 * 1024
        ),
    )(
        idx,
        flags,
        bounds,
        frames.reshape(32, 16, D),
        cotangent.reshape(12, BLOCK, D),
        panel,
        kernel,
        norm_gain.reshape(CHUNKS, 128),
        norm_shift.reshape(CHUNKS, 128),
    )
    return (mapped, input_grad.reshape(SLOTS, D), *rest)


def solution(mesh):
    placed = (
        P(("dp", "fsdp"), None),
        P(None, ("dp", "fsdp")),
        P(None, "fsdp", None),
        P(),
        P(),
        P(),
        P("fsdp", None),
        P(("dp", "fsdp"), None),
    )
    return jax.shard_map(
        shards,
        mesh=mesh,
        in_specs=placed,
        out_specs=(P(("dp", "fsdp"), None), P(("dp", "fsdp"), None), P("fsdp", None), P(), P()),
        check_vma=False,
    )
```

time: 1050 us -> 195 us (0.19)
  waiting for transfers between devices: 633 us -> 0 us
  blocking collectives: 229 us -> 0 us
  Pallas kernels: 0 us -> 179 us
  other arithmetic: 90.5 us -> 3.43 us
  starting transfers between devices: 28 us -> 0 us
  matrix products: 22.9 us -> 0 us
  local copies, waits for them, and re-layouts: 25.9 us -> 9.75 us
  between operations: 16.6 us -> 1.98 us
    psum x2 -> x0, waiting for transfers between devices: 259 us -> none  [the longest x1 144 us: shards(): panel_grad = lax.psum(partial_grad, 'dp')]
    psum x3 -> x0, blocking collectives: 229 us -> none  [the longest x1 98.3 us: shards(): lax.psum((jnp.sum(normed_grad * whitened, axis=0), jnp.sum(normed_grad, a...]
    reduce_scatter x1 -> x0, waiting for transfers between devices: 191 us -> none  [shards(): lax.psum_scatter(lax.dot_general(columns, cotangent, (((0,), (0,)), ((),...]
    pallas_call x0 -> x1, Pallas kernels: none -> 179 us  [shards(): pl.pallas_call(fused, out_shape=(shape((ROWS, D), BF16), shape((32, 16, D...]
    all_gather x1 -> x0, waiting for transfers between devices: 150 us -> none  [shards(): lax.all_gather(panel, 'fsdp', axis=0, tiled=True)]
    reduce_sum x7 -> x3, other arithmetic: 45.4 us -> 1.6 us  [the longest x1 1.3 us: routing(): blocks = jnp.sum((mine_row >= 0).astype(jnp.int32))]
    all_to_all x2 -> x0, waiting for transfers between devices: 28.2 us -> none  [the longest x1 28.2 us: shards(): lax.all_to_all(outgoing, 'dp', split_axis=0, concat_axis=0, tiled=True)]
    convert_element_type x3 -> x1, other arithmetic: 23.1 us -> 0.08 us  [routing(): flags = jnp.concatenate([labels < blocks, labels + 1 == blocks]).astype(F32)]
  transfers between devices with their start and end apart: 10 -> 0, of which waited for: 6 -> 0; matrix products, arithmetic and copies ran while one was open for 9% -> 0% of each run, Pallas kernels for 0% -> 0%
where the time goes in v1:
time: 195 us; the launch traced here: 194 us
  Pallas kernels  179 us (92%)
  local copies, waits for them, and re-layouts  9.75 us (5%)
  other arithmetic  3.43 us (2%)
  between operations  1.98 us (1%)
    pallas_call x1, Pallas kernels, shards(): pl.pallas_call(fused, out_shape=(shape((ROWS, D), BF16), shape((32, 16, D...  179 us
    unnamed x13, local copies, waits for them, and re-layouts  7.81 us

profile of v1, /device:TPU:1, one launch (start us, length us, event | category | flops | bytes accessed | tf_op | source)
XLA Modules:
  0.0 194.5 jit_solution(15098497423037060259)
XLA Ops:
  0.6 1.1 compare_reduce_fusion
  1.7 1.3 fusion.3
  4.3 0.2 convert_reduce_fusion
  4.5 0.1 select_reduce_fusion
  4.7 1.2 concatenate.15.idx
  5.9 0.7 add_compare_fusion
  6.6 0.1 add_convert_fusion
  6.6 0.7 concatenate.18.flags
  7.3 179.3 %shard_map.119 = (bf16[384,2048]{1,0:T(8,128)(2,1)}, bf16[32,16,2048]{2,1,0:T(8,128)(2,1)}, f32[256,2048]{1,0:T(8,128)}, f32[9,2048]{1,0:T(8,128)}, f32[2,2048]{1,0:T(2,128)}) custom-call(s32[64]{0:T(128)} %concatenate.15.idx, f32[40,128]{1,0:T(8,128)} %concatenate.18.flags, s32[2,512]{1,0:T(2,128)} %bounds.1, bf16[32,16,2048]{2,1,0:T(8,128)(2,1)} %bitcast.12, ...), custom_call_target="tpu_custom_call" | custom-call | tf_op jit(solution)/shard_map/pallas_call | solution.py:728
  186.7 0.0 copy-start.1
  186.7 2.9 %copy.18 = bf16[384,2048]{1,0:T(8,128)(2,1)} copy(bf16[384,2048]{1,0:T(8,128)(2,1)} %get-tuple-element.29) | data formatting | bytes 3145728
  189.5 0.0 copy-done.1
  189.5 0.0 copy-start
  189.5 1.3 copy.19
  190.9 1.0 copy-done
  191.9 0.0 copy-start.2
  191.9 0.0 copy-start.3
  191.9 1.3 copy.20
  193.2 0.0 copy-done.2
  193.2 0.7 copy.21
  193.9 0.0 copy-done.3
  193.9 0.6 copy.22
  (4 shorter events, 0.0 us)
Async XLA Ops:
  186.7 2.9 %copy-start.1 = (bf16[32,16,2048]{2,1,0:T(8,128)(2,1)S(1)}, bf16[32,16,2048]{2,1,0:T(8,128)(2,1)}, u32[]{:S(2)}) copy-start(bf16[32,16,2048]{2,1,0:T(8,128)(2,1)} %get-tuple-element.11) | copy-start | bytes 6291460
  189.5 2.3 %copy-start = (f32[256,2048]{1,0:T(8,128)S(1)}, f32[256,2048]{1,0:T(8,128)}, u32[]{:S(2)}) copy-start(f32[256,2048]{1,0:T(8,128)} %get-tuple-element.31) | copy-start | bytes 6291460
  191.9 1.3 copy-start.2
  191.9 2.0 %copy-start.3 = (f32[2,2048]{1,0:T(2,128)S(1)}, f32[2,2048]{1,0:T(2,128)}, u32[]{:S(2)}) copy-start(f32[2,2048]{1,0:T(2,128)} %get-tuple-element.33) | copy-start | bytes 49156

commit v2 on v1

--- a/solution.py
+++ b/solution.py
@@ -23,11 +23,27 @@
 RANK, DEST, SEND, PICK, LIVE = 0, 16, 32, 48, 60
 
 
+def peer_at(dp, slot):
+    return (
+        ((dp // 4 + slot // 4) % 4) * 4
+        + ((dp // 2 + slot // 2) % 2) * 2
+        + (dp + slot) % 2
+    )
+
+
+def slot_of(dp, source):
+    return (
+        ((dp // 4 - source // 4 + 4) % 4) * 4
+        + ((dp // 2 + source // 2) % 2) * 2
+        + (dp + source) % 2
+    )
+
+
 def routing(destinations, data_index):
     plan_table = destinations[:, 0, :]
     mine_row = lax.dynamic_index_in_dim(plan_table, data_index, 0, keepdims=False)
     labels = jnp.arange(N_DP, dtype=jnp.int32)
-    peers = (data_index + labels) % N_DP
+    peers = peer_at(data_index, labels)
     send_match = mine_row[None, :] == peers[:, None]
     send_row = jnp.sum(jnp.where(send_match, labels[None, :], 0), axis=1)
     arrives = jnp.any(plan_table == data_index, axis=1)
@@ -36,9 +52,9 @@
     source_rank = jnp.sum(((labels[None, :] < labels[:, None]) & arrives[None, :]).astype(jnp.int32), axis=1)
     wanted = jnp.arange(12, dtype=jnp.int32)
     chosen = arrives[None, :] & (source_rank[None, :] == wanted[:, None])
-    source_slot = (data_index - labels + N_DP) % N_DP
+    source_slot = slot_of(data_index, labels)
     pick_slot = jnp.sum(jnp.where(chosen, source_slot[None, :], 0), axis=1)
-    back_slot = jnp.where(mine_row >= 0, (data_index - mine_row + N_DP) % N_DP, 0)
+    back_slot = jnp.where(mine_row >= 0, slot_of(data_index, jnp.maximum(mine_row, 0)), 0)
     blocks = jnp.sum((mine_row >= 0).astype(jnp.int32))
     tail = jnp.stack([BLOCK * blocks, 2 * blocks - 1, BLOCK * blocks - 8, blocks])
     idx = jnp.concatenate(
@@ -74,7 +90,7 @@
 S_NG1 = SEMS.take(8)
 S_NG2 = SEMS.take(16)
 S_BHALO = SEMS.take(4)
-S_R1 = SEMS.take(4)
+S_R1 = SEMS.take(6)
 S_R2 = SEMS.take(4)
 S_R3 = SEMS.take(4)
 S_GAT = SEMS.take(8)
@@ -116,6 +132,7 @@
     atp,
     gp,
     r1,
+    rd,
     s1,
     r2,
     s2,
@@ -204,8 +221,6 @@
             keep = (before >= float(max(-o, 0))) & (after >= float(max(o, 0)))
             msk[tap, part, :] = jnp.where(keep, 1.0, 0.0)
 
-    pl.semaphore_wait(barrier, 25)
-
     def unit(f_of):
         return pan.at[pl.ds(pl.multiple_of(f_of * 256 + c * 128, 128), 128)]
 
@@ -247,38 +262,60 @@
 
     load_frames.wait()
     htrail[...] = fr[idx[LIVE + 1]]
+
+    def widen(j):
+        for q in range(4):
+            part = fr[8 * q : 8 * q + 8, :, lanes(j)].reshape(128, 128)
+            ext[j, 8 + 128 * q : 136 + 128 * q, :] = part.astype(F32)
+        ext[j, 0:8, :] = jnp.zeros((8, 128), F32)
+        ext[j, 520:528, :] = jnp.zeros((8, 128), F32)
+
+    loop(CHUNKS, widen)
+
+    def conv_at(j, base, count, taps):
+        accum = jnp.zeros((count, 128), F32)
+        for tap in range(TAPS):
+            window = ext[j, pl.ds(base + 4 + tap, count), :] * taps[tap : tap + 1]
+            accum = accum + msk[tap, pl.ds(base, count), :] * window
+        filt[j, pl.ds(base, count), :] = accum
+
+    def conv(j):
+        taps = kern[:, lanes(j)]
+        loop(8, lambda i: conv_at(j, pl.multiple_of(i * 64, 64), 64, taps))
+
+    loop(CHUNKS, conv)
+
+    load_cot.wait()
+    load_panel.wait()
+    pl.semaphore_wait(barrier, 25)
+
     halo_next = remote(htrail, hprev, S_HALO, follow // N_FSDP, follow % N_FSDP)
     halo_prev = remote(fr.at[0], hnext, S_HALO + 1, lead // N_FSDP, lead % N_FSDP)
     halo_next.start()
     halo_prev.start()
-
-    load_panel.wait()
     for copy in own_copies:
         copy.start()
 
-    load_cot.wait()
-
-    def cot_block(k):
-        return cot[idx[RANK + k]]
-
-    cr[0] = cot_block(0)
+    def same_z(m):
+        return (m // 2) * 4 + m % 2
+
+    def other_z(m):
+        return (m // 2) * 4 + m % 2 + 2
 
     def cot_copy(k):
-        return remote(cs.at[k], cr.at[k], S_COT + k, (dp + k) % N_DP, f)
+        return remote(cs.at[k], cr.at[k], S_COT + k, peer_at(dp, k), f)
 
     def send_cot(k):
-        cs[k] = cot_block(k)
+        cs[k] = cot[idx[RANK + k]]
         cot_copy(k).start()
 
-    loop(N_DP, send_cot, 1)
-
-    def widen(j):
-        for q in range(4):
-            part = fr[8 * q : 8 * q + 8, :, lanes(j)].reshape(128, 128)
-            ext[j, 8 + 128 * q : 136 + 128 * q, :] = part.astype(F32)
-        ext[j, 520:528, :] = jnp.zeros((8, 128), F32)
-
-    loop(CHUNKS, widen)
+    cr[0] = cot[idx[RANK]]
+    loop(8, lambda m: send_cot(same_z(m)), 1)
+
+    def fill_cot(k):
+        cs[k] = cot[idx[RANK + k]]
+
+    loop(8, lambda m: fill_cot(other_z(m)))
 
     halo_next.wait_recv()
     halo_prev.wait_recv()
@@ -291,45 +328,35 @@
             last = flags[15 + b : 16 + b, :]
             ref[j, at_row : at_row + 8, :] = here * (1.0 - last) + following * last
 
-    def place_frames(j):
+    def fold(value):
+        return jnp.sum(value, axis=0, keepdims=True)
+
+    def edges(j):
         place(
             ext,
             j,
             hprev[:, lanes(j)].astype(F32)[8:16],
             hnext[:, lanes(j)].astype(F32)[0:8],
         )
-
-    loop(CHUNKS, place_frames)
-
-    def fold(value):
-        return jnp.sum(value, axis=0, keepdims=True)
-
-    def conv(j):
         taps = kern[:, lanes(j)]
-
-        def part(i, total):
-            base = i * 64
-            accum = jnp.zeros((64, 128), F32)
-            for tap in range(TAPS):
-                window = ext[j, pl.ds(base + 4 + tap, 64), :] * taps[tap : tap + 1]
-                accum = accum + msk[tap, rows(base, 64), :] * window
-            filt[j, rows(base, 64), :] = accum
-            return total + jnp.sum(accum.reshape(8, 8, 128), axis=0)
-
-        total = lax.fori_loop(0, 8, part, jnp.zeros((8, 128), F32))
+        conv_at(j, 0, 8, taps)
+        for b in range(8, 17):
+            conv_at(j, BLOCK * b - 8, 8, taps)
+
+        total = jnp.zeros((8, 128), F32)
+        for q in range(8):
+            part = filt[j, 64 * q : 64 * q + 64, :]
+            total = total + jnp.sum(part.reshape(8, 8, 128), axis=0)
         total = fold(total)
         mean = total / flags[32:33, :]
-
-        def spread(i, total):
-            base = i * 64
-            off = (filt[j, rows(base, 64), :] - mean) * msk[4, rows(base, 64), :]
-            return total + jnp.sum((off * off).reshape(8, 8, 128), axis=0)
-
-        squares = fold(lax.fori_loop(0, 8, spread, jnp.zeros((8, 128), F32)))
+        squares = jnp.zeros((8, 128), F32)
+        for q in range(8):
+            off = (filt[j, 64 * q : 64 * q + 64, :] - mean) * msk[4, 64 * q : 64 * q + 64, :]
+            squares = squares + jnp.sum((off * off).reshape(8, 8, 128), axis=0)
         st1[0, pl.ds(j, 1), :] = total
-        st1[0, pl.ds(16 + j, 1), :] = squares
-
-    loop(CHUNKS, conv)
+        st1[0, pl.ds(16 + j, 1), :] = fold(squares)
+
+    loop(CHUNKS, edges)
     st1[0, 32:40, :] = flags[32:40, :]
 
     def over_fsdp(buf, sem):
@@ -386,6 +413,7 @@
     fwd_copies[0].start()
     fwd_copies[1].start()
     pair_copies[0].start()
+    loop(8, lambda m: cot_copy(other_z(m)).start())
     own_copies[1].wait_recv()
     far_copies[0].start()
     pair_copies[1].start()
@@ -400,12 +428,40 @@
     st2[0, 32:40, :] = number
     begin(copy_st2, N_DP)
 
+    arrive(copy_st2, N_DP)
+    sums, squares, number = merge(st2, N_DP, dp)
+    stat[0:16, :] = sums / TOTAL
+    stat[16:32, :] = lax.rsqrt(squares / TOTAL + EPSILON)
+
+    def activate(j):
+        average = stat[pl.ds(j, 1), :]
+        inverse = stat[pl.ds(16 + j, 1), :]
+        g = gain[pl.ds(j, 1), :]
+        b = shift[pl.ds(j, 1), :]
+        for q in range(4):
+            base = 128 * q
+            keep = msk[4, base : base + 128, :]
+            whitened = (filt[j, base : base + 128, :] - average) * inverse
+            normed = whitened * g + b
+            logistic = 1.0 / (1.0 + jnp.exp(-normed))
+            value = normed * logistic * keep
+            filt[j, base : base + 128, :] = whitened
+            act[4 * q : 4 * q + 4, :, lanes(j)] = value.astype(BF16).reshape(4, BLOCK, 128)
+            at[j % 2, rows((j // 2) * 128, 128), base : base + 128] = value.T.astype(BF16)
+
+    loop(CHUNKS, activate)
+    copy_at = remote(at.at[1 - c], atp, S_AT, partner, f)
+    copy_at.start()
+
     fwd_copies[0].wait_recv()
     far_copies[2].start()
     pair_copies[3].start()
     fwd_copies[1].wait_recv()
     far_copies[3].start()
     pair_copies[4].start()
+    far_copies[0].wait_recv()
+    far_copies[1].wait_recv()
+    pair_copies[5].start()
 
     loop(N_DP, lambda k: cot_copy(k).wait_recv(), 1)
 
@@ -418,10 +474,70 @@
     copy_cp = remote(cp, cpp, S_CP, partner, f)
     copy_cp.start()
 
-    arrive(copy_st2, N_DP)
-    sums, squares, number = merge(st2, N_DP, dp)
-    stat[0:16, :] = sums / TOTAL
-    stat[16:32, :] = lax.rsqrt(squares / TOTAL + EPSILON)
+    ar[0] = act[idx[SEND]]
+
+    def act_copy(k):
+        return remote(cs.at[k], ar.at[k], S_ACT + k, peer_at(dp, k), f)
+
+    def send_act(k):
+        cot_copy(k).wait_send()
+        cs[k] = act[idx[SEND + k]]
+        act_copy(k).start()
+
+    loop(N_DP, send_act, 1)
+
+    up, down, across = (y + 1) % 4, (y + 3) % 4, (y + 2) % 4
+    f_above, f_below = up * 2 + zl, down * 2 + zl
+
+    def half(ref, h):
+        return ref.at[pl.ds(2 * h, 2)]
+
+    across_up = remote(half(gp.at[across], 0), rd.at[0], S_R1, dp, f_above)
+    across_down = remote(half(gp.at[across], 1), rd.at[1], S_R1 + 1, dp, f_below)
+    plain_up = remote(half(gp.at[up], 1), half(r1.at[0], 1), S_R1 + 2, dp, f_above)
+    plain_down = remote(half(gp.at[down], 0), half(r1.at[1], 0), S_R1 + 3, dp, f_below)
+    added_up = remote(half(gp.at[up], 0), half(r1.at[0], 0), S_R1 + 4, dp, f_above)
+    added_down = remote(half(gp.at[down], 1), half(r1.at[1], 1), S_R1 + 5, dp, f_below)
+
+    def copy_r2(k):
+        b = (x + k) % 4
+        return remote(s1.at[b], r2.at[k - 1], S_R2 + k, b * 4 + zh * 2 + c, f)
+
+    def copy_r3(k):
+        to_z = (z + k) % 4
+        return remote(
+            s2.at[to_z], r3.at[k - 1], S_R3 + k, x * 4 + (to_z // 2) * 2 + c, y * 2 + to_z % 2
+        )
+
+    def products(a):
+        def product(b):
+            d_rows = rows(a * 256, 256)
+            columns = pl.ds(pl.multiple_of(b * 512, 512), 512)
+            value = jnp.dot(at[c, d_rows, :], cp[:, columns], preferred_element_type=F32)
+            value = value + jnp.dot(
+                atp[d_rows, :], cpp[:, columns], preferred_element_type=F32
+            )
+            for h in range(2):
+                for low in range(2):
+                    piece = value[low * 128 : low * 128 + 128, h * 256 : h * 256 + 256]
+                    gp[a, b, h * 2 + low] = piece.astype(BF16)
+
+        loop(4, product)
+
+    copy_at.wait_recv()
+    copy_cp.wait_recv()
+    products(across)
+    across_up.start()
+    across_down.start()
+    far_copies[2].wait_recv()
+    far_copies[3].wait_recv()
+    pair_copies[6].start()
+    products(up)
+    plain_up.start()
+    products(down)
+    plain_down.start()
+    for copy in pair_copies:
+        copy.wait_recv()
 
     def act_grad(f_of):
         value = lax.dot_general(
@@ -434,36 +550,21 @@
         ngx[f_of * 2, 8:520, :] = value[:, 0:128]
         ngx[f_of * 2 + 1, 8:520, :] = value[:, 128:256]
 
-    far_copies[0].wait_recv()
-    far_copies[1].wait_recv()
-    pair_copies[5].start()
-    far_copies[2].wait_recv()
-    far_copies[3].wait_recv()
-    pair_copies[6].start()
-    for copy in pair_copies:
-        copy.wait_recv()
     loop(N_FSDP, act_grad)
 
-    def activate(j):
-        average = stat[pl.ds(j, 1), :]
-        inverse = stat[pl.ds(16 + j, 1), :]
+    def slopes(j):
         g = gain[pl.ds(j, 1), :]
         b = shift[pl.ds(j, 1), :]
         sum_w = jnp.zeros((8, 128), F32)
         sum_1 = jnp.zeros((8, 128), F32)
         for q in range(4):
             base = 128 * q
-            keep = msk[4, base : base + 128, :]
-            whitened = (filt[j, base : base + 128, :] - average) * inverse
+            whitened = filt[j, base : base + 128, :]
             normed = whitened * g + b
             logistic = 1.0 / (1.0 + jnp.exp(-normed))
-            value = normed * logistic * keep
             slope = logistic + normed * logistic * (1.0 - logistic)
             grad = ngx[j, 8 + base : 136 + base, :] * slope
-            filt[j, base : base + 128, :] = whitened
             ngx[j, 8 + base : 136 + base, :] = grad
-            act[4 * q : 4 * q + 4, :, lanes(j)] = value.astype(BF16).reshape(4, BLOCK, 128)
-            at[j % 2, rows((j // 2) * 128, 128), base : base + 128] = value.T.astype(BF16)
             sum_w = sum_w + jnp.sum((grad * whitened).reshape(16, 8, 128), axis=0)
             sum_1 = sum_1 + jnp.sum(grad.reshape(16, 8, 128), axis=0)
         ng1[0, pl.ds(j, 1), :] = fold(sum_w)
@@ -473,7 +574,7 @@
         bsend[2, j] = ngx[j, pl.ds(idx[LIVE], 8), :]
         bsend[3, j] = filt[j, pl.ds(idx[LIVE + 2], 8), :]
 
-    loop(CHUNKS, activate)
+    loop(CHUNKS, slopes)
 
     copy_ng1 = over_fsdp(ng1, S_NG1)
     copy_ng2 = over_dp(ng2, S_NG2)
@@ -486,73 +587,26 @@
     ]
     for copy in halo_copies:
         copy.start()
-    copy_at = remote(at.at[1 - c], atp, S_AT, partner, f)
-    copy_at.start()
-
-    def act_block(k):
-        return act[idx[SEND + k]]
-
-    ar[0] = act_block(0)
-
-    def act_copy(k):
-        return remote(cs.at[k], ar.at[k], S_ACT + k, (dp + k) % N_DP, f)
-
-    def send_act(k):
-        cot_copy(k).wait_send()
-        cs[k] = act_block(k)
-        act_copy(k).start()
-
-    loop(N_DP, send_act, 1)
+
+    def pass_on(a, h, n):
+        def add(i):
+            b, m = i // 4, i % 4
+            value = gp[a, 2 * h + b, m].astype(F32) + rd[n, b, m].astype(F32)
+            gp[a, 2 * h + b, m] = value.astype(BF16)
+
+        loop(8, add)
+
+    across_up.wait_recv()
+    pass_on(up, 0, 0)
+    added_up.start()
+    across_down.wait_recv()
+    pass_on(down, 1, 1)
+    added_down.start()
 
     arrive(copy_ng1, N_FSDP)
     ng2[0] = ordered(ng1, N_FSDP, f, (32, 128))
     begin(copy_ng2, N_DP)
-
-    copy_cp.wait_recv()
-    copy_at.wait_recv()
-    first = y * (1 - c) + x * c
-    second = x * (1 - c) + y * c
-
-    def first_peer(a):
-        return ((x * (1 - c) + a * c) * 4 + zh * 2 + c, (a * (1 - c) + y * c) * 2 + zl)
-
-    def second_peer(b):
-        return ((b * (1 - c) + x * c) * 4 + zh * 2 + c, (y * (1 - c) + b * c) * 2 + zl)
-
-    def copy_r1(k):
-        a = (first + k) % 4
-        return remote(gp.at[a], r1.at[k - 1], S_R1 + k, *first_peer(a))
-
-    def copy_r2(k):
-        b = (second + k) % 4
-        return remote(s1.at[b], r2.at[k - 1], S_R2 + k, *second_peer(b))
-
-    def copy_r3(k):
-        to_z = (z + k) % 4
-        return remote(
-            s2.at[to_z], r3.at[k - 1], S_R3 + k, x * 4 + (to_z // 2) * 2 + c, y * 2 + to_z % 2
-        )
-
-    for k in (1, 2, 3, 4):
-        a = (first + k) % 4
-
-        def product(b, a=a):
-            y_of = a * (1 - c) + b * c
-            x_of = b * (1 - c) + a * c
-            d_rows = rows(y_of * 256, 256)
-            columns = pl.ds(pl.multiple_of(x_of * 512, 512), 512)
-            value = jnp.dot(at[c, d_rows, :], cp[:, columns], preferred_element_type=F32)
-            value = value + jnp.dot(
-                atp[d_rows, :], cpp[:, columns], preferred_element_type=F32
-            )
-            for h in range(2):
-                for low in range(2):
-                    piece = value[low * 128 : low * 128 + 128, h * 256 : h * 256 + 256]
-                    gp[a, b, h * 2 + low] = piece.astype(BF16)
-
-        loop(4, product)
-        if k < 4:
-            copy_r1(k).start()
+    products(y)
 
     arrive(copy_ng2, N_DP)
     ng_total = ordered(ng2, N_DP, dp, (32, 128))
@@ -614,13 +668,13 @@
     begin(copy_k1, N_DP)
     kg1[0] = kg[dp]
 
-    for k in (1, 2, 3):
-        copy_r1(k).wait_recv()
+    for copy in (plain_up, plain_down, added_up, added_down):
+        copy.wait_recv()
 
     def add_first(b):
         for n in range(4):
-            value = gp[first, b, n].astype(F32)
-            for k in range(3):
+            value = gp[y, b, n].astype(F32)
+            for k in range(2):
                 value = value + r1[k, b, n].astype(F32)
             s1[b, n] = value.astype(BF16)
 
@@ -651,10 +705,10 @@
         copy_r2(k).wait_recv()
 
     def add_second(n):
-        value = s1[second, n].astype(F32)
+        value = s1[x, n].astype(F32)
         for k in range(3):
             value = value + r2[k, n].astype(F32)
-        s2[n] = value.astype(BF16)
+        s2[n] = value
 
     loop(4, add_second)
     for k in (1, 2, 3):
@@ -674,9 +728,9 @@
 
     for k in (1, 2, 3):
         copy_r3(k).wait_recv()
-    value = s2[z].astype(F32)
+    value = s2[z]
     for k in range(3):
-        value = value + r3[k].astype(F32)
+        value = value + r3[k]
     place_of = x * 2 + zh
     pgb[c, place_of] = value.astype(BF16)
 
@@ -706,9 +760,10 @@
         copy.wait_send()
     copy_cp.wait_send()
     copy_at.wait_send()
+    for copy in (across_up, across_down, plain_up, plain_down, added_up, added_down):
+        copy.wait_send()
     copy_gpair.wait_send()
     for k in (1, 2, 3):
-        copy_r1(k).wait_send()
         copy_r2(k).wait_send()
         copy_r3(k).wait_send()
     for copy in (copy_st2, act_copy, copy_ng2, copy_k1, copy_k3):
@@ -753,11 +808,12 @@
             pltpu.VMEM((2, 1024, 512), BF16),
             pltpu.VMEM((1024, 512), BF16),
             pltpu.VMEM((4, 4, 4, 128, 256), BF16),
-            pltpu.VMEM((3, 4, 4, 128, 256), BF16),
+            pltpu.VMEM((2, 4, 4, 128, 256), BF16),
+            pltpu.VMEM((2, 2, 4, 128, 256), BF16),
             pltpu.VMEM((4, 4, 128, 256), BF16),
             pltpu.VMEM((3, 4, 128, 256), BF16),
-            pltpu.VMEM((4, 128, 256), BF16),
-            pltpu.VMEM((3, 128, 256), BF16),
+            pltpu.VMEM((4, 128, 256), F32),
+            pltpu.VMEM((3, 128, 256), F32),
             pltpu.VMEM((2, 8, 128, 256), BF16),
             pltpu.VMEM((256, D), F32),
             pltpu.VMEM((ROWS, D), BF16),

time: 195 us -> 183 us (0.938)
  Pallas kernels: 179 us -> 167 us
    pallas_call x1, Pallas kernels: 179 us -> 167 us  [shards(): pl.pallas_call(fused, out_shape=(shape((ROWS, D), BF16), shape((32, 16, D...]
where the time goes in v2:
time: 183 us
  Pallas kernels  167 us (91%)
  local copies, waits for them, and re-layouts  9.75 us (5%)
  other arithmetic  3.44 us (2%)
  between operations  2 us (1%)
    pallas_call x1, Pallas kernels, shards(): pl.pallas_call(fused, out_shape=(shape((ROWS, D), BF16), shape((32, 16, D...  167 us
    unnamed x13, local copies, waits for them, and re-layouts  7.81 us

profile of v2, /device:TPU:1, one launch (start us, length us, event | category | flops | bytes accessed | tf_op | source)
XLA Modules:
  0.0 182.5 jit_solution(4497976408640961653)
XLA Ops:
  0.7 1.1 compare_reduce_fusion
  1.8 1.3 fusion.5
  4.4 0.2 convert_reduce_fusion
  4.6 0.1 select_reduce_fusion
  4.7 1.2 concatenate.15.idx
  5.9 0.7 add_compare_fusion
  6.6 0.1 add_convert_fusion
  6.7 0.7 concatenate.18.flags
  7.4 167.3 %shard_map.119 = (bf16[384,2048]{1,0:T(8,128)(2,1)}, bf16[32,16,2048]{2,1,0:T(8,128)(2,1)}, f32[256,2048]{1,0:T(8,128)}, f32[9,2048]{1,0:T(8,128)}, f32[2,2048]{1,0:T(2,128)}) custom-call(s32[64]{0:T(128)} %concatenate.15.idx, f32[40,128]{1,0:T(8,128)} %concatenate.18.flags, s32[2,512]{1,0:T(2,128)} %bounds.1, bf16[32,16,2048]{2,1,0:T(8,128)(2,1)} %bitcast.12, ...), custom_call_target="tpu_custom_call" | custom-call | tf_op jit(solution)/shard_map/pallas_call | solution.py:783
  174.7 0.0 copy-start.1
  174.7 2.9 %copy.18 = bf16[384,2048]{1,0:T(8,128)(2,1)} copy(bf16[384,2048]{1,0:T(8,128)(2,1)} %get-tuple-element.29) | data formatting | bytes 3145728
  177.6 0.0 copy-done.1
  177.6 0.0 copy-start
  177.6 1.3 copy.19
  178.9 1.0 copy-done
  179.9 0.0 copy-start.2
  179.9 0.0 copy-start.3
  179.9 1.3 copy.20
  181.3 0.0 copy-done.2
  181.3 0.7 copy.21
  181.9 0.0 copy-done.3
  181.9 0.6 copy.22
  (4 shorter events, 0.0 us)
Async XLA Ops:
  174.7 2.9 %copy-start.1 = (bf16[32,16,2048]{2,1,0:T(8,128)(2,1)S(1)}, bf16[32,16,2048]{2,1,0:T(8,128)(2,1)}, u32[]{:S(2)}) copy-start(bf16[32,16,2048]{2,1,0:T(8,128)(2,1)} %get-tuple-element.11) | copy-start | bytes 6291460
  177.6 2.3 %copy-start = (f32[256,2048]{1,0:T(8,128)S(1)}, f32[256,2048]{1,0:T(8,128)}, u32[]{:S(2)}) copy-start(f32[256,2048]{1,0:T(8,128)} %get-tuple-element.31) | copy-start | bytes 6291460
  179.9 1.3 copy-start.2
  179.9 2.0 %copy-start.3 = (f32[2,2048]{1,0:T(2,128)S(1)}, f32[2,2048]{1,0:T(2,128)}, u32[]{:S(2)}) copy-start(f32[2,2048]{1,0:T(2,128)} %get-tuple-element.33) | copy-start | bytes 49156

commit v3 on v2

--- a/solution.py
+++ b/solution.py
@@ -138,7 +138,6 @@
     s2,
     r3,
     pgb,
-    pst,
     mst,
     htrail,
     hprev,
@@ -312,10 +311,7 @@
     cr[0] = cot[idx[RANK]]
     loop(8, lambda m: send_cot(same_z(m)), 1)
 
-    def fill_cot(k):
-        cs[k] = cot[idx[RANK + k]]
-
-    loop(8, lambda m: fill_cot(other_z(m)))
+    loop(8, lambda m: send_cot(other_z(m)))
 
     halo_next.wait_recv()
     halo_prev.wait_recv()
@@ -413,7 +409,6 @@
     fwd_copies[0].start()
     fwd_copies[1].start()
     pair_copies[0].start()
-    loop(8, lambda m: cot_copy(other_z(m)).start())
     own_copies[1].wait_recv()
     far_copies[0].start()
     pair_copies[1].start()
@@ -459,9 +454,6 @@
     fwd_copies[1].wait_recv()
     far_copies[3].start()
     pair_copies[4].start()
-    far_copies[0].wait_recv()
-    far_copies[1].wait_recv()
-    pair_copies[5].start()
 
     loop(N_DP, lambda k: cot_copy(k).wait_recv(), 1)
 
@@ -485,6 +477,10 @@
         act_copy(k).start()
 
     loop(N_DP, send_act, 1)
+
+    far_copies[0].wait_recv()
+    far_copies[1].wait_recv()
+    pair_copies[5].start()
 
     up, down, across = (y + 1) % 4, (y + 3) % 4, (y + 2) % 4
     f_above, f_below = up * 2 + zl, down * 2 + zl
@@ -657,16 +653,7 @@
             kg[j, tap : tap + 1, :] = fold(sums[tap])
 
     halo_prev.wait_send()
-    loop(CHUNKS, back)
-    store_igrad = pltpu.make_async_copy(fr, igrad, lsem.at[0])
-    store_igrad.start()
-
-    def copy_k1(k):
-        peer = (dp + k) % N_DP
-        return remote(kg.at[peer], kg1.at[k], S_K1 + k, peer, f)
-
-    begin(copy_k1, N_DP)
-    kg1[0] = kg[dp]
+    loop(8, back)
 
     for copy in (plain_up, plain_down, added_up, added_down):
         copy.wait_recv()
@@ -681,6 +668,17 @@
     loop(4, add_first)
     for k in (1, 2, 3):
         copy_r2(k).start()
+
+    loop(CHUNKS, back, 8)
+    store_igrad = pltpu.make_async_copy(fr, igrad, lsem.at[0])
+    store_igrad.start()
+
+    def copy_k1(k):
+        peer = (dp + k) % N_DP
+        return remote(kg.at[peer], kg1.at[k], S_K1 + k, peer, f)
+
+    begin(copy_k1, N_DP)
+    kg1[0] = kg[dp]
 
     arrive(copy_k1, N_DP)
     kg2[0] = ordered(kg1, N_DP, dp, (16, 128))
@@ -749,10 +747,7 @@
         kgrad[:, 128 * j : 128 * j + 128] = kg3[j, 0:TAPS, :]
 
     copy_gpair.wait_recv()
-    for u in range(8):
-        pst[0:128, 256 * u : 256 * u + 256] = pgb[0, u].astype(F32)
-        pst[128:256, 256 * u : 256 * u + 256] = pgb[1, u].astype(F32)
-    store_pgrad = pltpu.make_async_copy(pst, pgrad, lsem.at[2])
+    store_pgrad = pltpu.make_async_copy(pgb, pgrad, lsem.at[2])
     store_pgrad.start()
 
     halo_next.wait_send()
@@ -775,6 +770,24 @@
     store_pgrad.wait()
 
 
+def finish(mapped, igrad, pieces, kgrad, ngrad, o_mapped, o_igrad, o_pgrad, o_kgrad, o_ngrad, sems):
+    copies = [
+        pltpu.make_async_copy(source, target, sems.at[n])
+        for n, (source, target) in enumerate(
+            [(igrad, o_igrad), (mapped, o_mapped), (kgrad, o_kgrad), (ngrad, o_ngrad)]
+        )
+    ]
+    for copy in copies:
+        copy.start()
+    for half in range(2):
+        for u in range(8):
+            o_pgrad[128 * half : 128 * half + 128, 256 * u : 256 * u + 256] = pieces[
+                half, u
+            ].astype(F32)
+    for copy in copies:
+        copy.wait()
+
+
 def shards(frames, bounds, destinations, kernel, norm_gain, norm_shift, panel, cotangent):
     idx, flags = routing(destinations, lax.axis_index("dp"))
     hbm = pl.BlockSpec(memory_space=pl.ANY)
@@ -785,7 +798,7 @@
         out_shape=(
             shape((ROWS, D), BF16),
             shape((32, 16, D), BF16),
-            shape((256, D), F32),
+            shape((2, 8, 128, 256), BF16),
             shape((TAPS, D), F32),
             shape((2, D), F32),
         ),
@@ -815,7 +828,6 @@
             pltpu.VMEM((4, 128, 256), F32),
             pltpu.VMEM((3, 128, 256), F32),
             pltpu.VMEM((2, 8, 128, 256), BF16),
-            pltpu.VMEM((256, D), F32),
             pltpu.VMEM((ROWS, D), BF16),
             pltpu.VMEM((16, D), BF16),
             pltpu.VMEM((16, D), BF16),
@@ -849,6 +861,21 @@
         norm_gain.reshape(CHUNKS, 128),
         norm_shift.reshape(CHUNKS, 128),
     )
+    results = (mapped, input_grad, *rest)
+    mapped, input_grad, *rest = pl.pallas_call(
+        finish,
+        out_shape=(
+            shape((ROWS, D), BF16),
+            shape((32, 16, D), BF16),
+            shape((256, D), F32),
+            shape((TAPS, D), F32),
+            shape((2, D), F32),
+        ),
+        in_specs=[hbm, hbm, vmem, hbm, hbm],
+        out_specs=(hbm, hbm, vmem, hbm, hbm),
+        scratch_shapes=[pltpu.SemaphoreType.DMA((4,))],
+        compiler_params=pltpu.CompilerParams(vmem_limit_bytes=60 * 1024 * 1024),
+    )(*results)
     return (mapped, input_grad.reshape(SLOTS, D), *rest)
 
 

time: 183 us -> 284 us (1.55)
  Pallas kernels: 167 us -> 277 us
  local copies, waits for them, and re-layouts: 9.75 us -> 1.93 us
    pallas_call x0 -> x1, Pallas kernels: none -> 119 us  [shards(): pl.pallas_call(finish, out_shape=(shape((ROWS, D), BF16), shape((32, 16,...]
    pallas_call x1, Pallas kernels: 167 us -> 157 us  [shards(): pl.pallas_call(fused, out_shape=(shape((ROWS, D), BF16), shape((32, 16, D...]
    unnamed x13 -> x0, local copies, waits for them, and re-layouts: 7.81 us -> none
where the time goes in v3:
time: 284 us
  Pallas kernels  277 us (98%)
  other arithmetic  3.44 us (1%)
    pallas_call x1, Pallas kernels, shards(): pl.pallas_call(fused, out_shape=(shape((ROWS, D), BF16), shape((32, 16, D...  157 us
    pallas_call x1, Pallas kernels, shards(): pl.pallas_call(finish, out_shape=(shape((ROWS, D), BF16), shape((32, 16,...  119 us

profile of v3, /device:TPU:1, one launch (start us, length us, event | category | flops | bytes accessed | tf_op | source)
XLA Modules:
  0.0 284.0 jit_solution(2361343324458546538)
XLA Ops:
  0.7 1.1 compare_reduce_fusion
  1.8 1.3 fusion.5
  4.4 0.2 convert_reduce_fusion
  4.6 0.1 select_reduce_fusion
  4.7 1.2 concatenate.15.idx
  5.9 0.7 add_compare_fusion
  6.6 0.1 add_convert_fusion
  6.7 0.7 concatenate.18.flags
  7.4 157.3 %shard_map.119 = (bf16[384,2048]{1,0:T(8,128)(2,1)}, bf16[32,16,2048]{2,1,0:T(8,128)(2,1)}, bf16[2,8,128,256]{3,2,1,0:T(8,128)(2,1)}, f32[9,2048]{1,0:T(8,128)}, f32[2,2048]{1,0:T(2,128)}) custom-call(s32[64]{0:T(128)} %concatenate.15.idx, f32[40,128]{1,0:T(8,128)} %concatenate.18.flags, s32[2,512]{1,0:T(2,128)} %bounds.1, bf16[32,16,2048]{2,1,0:T(8,128)(2,1)} %bitcast.12, ...), custom_call_target="tpu_custom_call" | custom-call | tf_op jit(solution)/shard_map/pallas_call | solution.py:796
  164.7 119.3 %shard_map.120 = (bf16[384,2048]{1,0:T(8,128)(2,1)}, bf16[32,16,2048]{2,1,0:T(8,128)(2,1)}, f32[256,2048]{1,0:T(8,128)}, f32[9,2048]{1,0:T(8,128)}, f32[2,2048]{1,0:T(2,128)}) custom-call(bf16[384,2048]{1,0:T(8,128)(2,1)} %get-tuple-element.15.mapped, bf16[32,16,2048]{2,1,0:T(8,128)(2,1)} %get-tuple-element.16.igrad, ...), custom_call_target="tpu_custom_call" | custom-call | tf_op jit(solution)/shard_map/pallas_call | solution.py:865
  (4 shorter events, 0.0 us)

commit v4 on v3

--- a/solution.py
+++ b/solution.py
@@ -39,30 +39,57 @@
     )
 
 
-def routing(destinations, data_index):
-    plan_table = destinations[:, 0, :]
-    mine_row = lax.dynamic_index_in_dim(plan_table, data_index, 0, keepdims=False)
-    labels = jnp.arange(N_DP, dtype=jnp.int32)
-    peers = peer_at(data_index, labels)
-    send_match = mine_row[None, :] == peers[:, None]
-    send_row = jnp.sum(jnp.where(send_match, labels[None, :], 0), axis=1)
-    arrives = jnp.any(plan_table == data_index, axis=1)
-    earlier = (labels[None, :] < peers[:, None]) & arrives[None, :]
-    rank_row = jnp.minimum(jnp.sum(earlier.astype(jnp.int32), axis=1), 11)
-    source_rank = jnp.sum(((labels[None, :] < labels[:, None]) & arrives[None, :]).astype(jnp.int32), axis=1)
-    wanted = jnp.arange(12, dtype=jnp.int32)
-    chosen = arrives[None, :] & (source_rank[None, :] == wanted[:, None])
-    source_slot = slot_of(data_index, labels)
-    pick_slot = jnp.sum(jnp.where(chosen, source_slot[None, :], 0), axis=1)
-    back_slot = jnp.where(mine_row >= 0, slot_of(data_index, jnp.maximum(mine_row, 0)), 0)
-    blocks = jnp.sum((mine_row >= 0).astype(jnp.int32))
-    tail = jnp.stack([BLOCK * blocks, 2 * blocks - 1, BLOCK * blocks - 8, blocks])
-    idx = jnp.concatenate(
-        [rank_row, back_slot, send_row, pick_slot, tail]
-    )
-    flags = jnp.concatenate([labels < blocks, labels + 1 == blocks]).astype(F32)
-    count = jnp.full((8, 128), (BLOCK * blocks).astype(F32))
-    return idx, jnp.concatenate([jnp.broadcast_to(flags[:, None], (32, 128)), count])
+def routing(dest, idx, flags):
+    dp = lax.axis_index("dp")
+    mine = [dest[dp, 0, b] for b in range(16)]
+    blocks = jnp.int32(0)
+    for b in range(16):
+        live = (mine[b] >= 0).astype(jnp.int32)
+        blocks = blocks + live
+        idx[DEST + b] = live * slot_of(dp, jnp.maximum(mine[b], 0))
+        flags[b : b + 1, :] = jnp.full((1, 128), live.astype(F32), F32)
+
+    def sends(k, carry):
+        peer = peer_at(dp, k)
+        block = jnp.int32(0)
+        for b in range(16):
+            block = jnp.where(mine[b] == peer, b, block)
+        idx[SEND + k] = block
+        return carry
+
+    lax.fori_loop(0, N_DP, sends, 0)
+
+    def ranks(source, count):
+        arrives = jnp.int32(0)
+        for b in range(16):
+            arrives = jnp.where(dest[source, 0, b] == dp, 1, arrives)
+        idx[64 + source] = jnp.minimum(count, 11)
+        idx[80 + source] = jnp.where(arrives == 1, count, -1)
+        return count + arrives
+
+    lax.fori_loop(0, N_DP, ranks, jnp.int32(0))
+
+    def by_slot(k, carry):
+        idx[RANK + k] = idx[64 + peer_at(dp, k)]
+        return carry
+
+    lax.fori_loop(0, N_DP, by_slot, 0)
+
+    def picks(wanted, carry):
+        slot = jnp.int32(0)
+        for source in range(N_DP):
+            slot = jnp.where(idx[80 + source] == wanted, slot_of(dp, source), slot)
+        idx[PICK + wanted] = slot
+        return carry
+
+    lax.fori_loop(0, 12, picks, 0)
+    for b in range(16):
+        last = (blocks == b + 1).astype(F32)
+        flags[16 + b : 17 + b, :] = jnp.full((1, 128), last, F32)
+    flags[32:40, :] = jnp.full((8, 128), (blocks * BLOCK).astype(F32), F32)
+    idx[LIVE] = BLOCK * blocks
+    idx[LIVE + 1] = 2 * blocks - 1
+    idx[LIVE + 2] = BLOCK * blocks - 8
 
 
 class Sems:
@@ -770,29 +797,53 @@
     store_pgrad.wait()
 
 
-def finish(mapped, igrad, pieces, kgrad, ngrad, o_mapped, o_igrad, o_pgrad, o_kgrad, o_ngrad, sems):
-    copies = [
+def finish(
+    mapped, igrad, pieces, kgrad, ngrad, o_mapped, o_igrad, o_pgrad, o_kgrad, o_ngrad,
+    v_mapped, v_igrad, v_pieces, v_pgrad, sems,
+):
+    loads = [
         pltpu.make_async_copy(source, target, sems.at[n])
         for n, (source, target) in enumerate(
-            [(igrad, o_igrad), (mapped, o_mapped), (kgrad, o_kgrad), (ngrad, o_ngrad)]
+            [(pieces, v_pieces), (igrad, v_igrad), (mapped, v_mapped)]
         )
     ]
-    for copy in copies:
+    for copy in loads:
         copy.start()
-    for half in range(2):
+    o_kgrad[...] = kgrad[...]
+    o_ngrad[...] = ngrad[...]
+    loads[0].wait()
+    stores = []
+    for part in range(2):
         for u in range(8):
-            o_pgrad[128 * half : 128 * half + 128, 256 * u : 256 * u + 256] = pieces[
-                half, u
+            v_pgrad[128 * part : 128 * part + 128, 256 * u : 256 * u + 256] = v_pieces[
+                part, u
             ].astype(F32)
-    for copy in copies:
+        half = pl.ds(128 * part, 128)
+        stores.append(
+            pltpu.make_async_copy(v_pgrad.at[half], o_pgrad.at[half], sems.at[3 + part])
+        )
+        stores[-1].start()
+    loads[1].wait()
+    stores.append(pltpu.make_async_copy(v_igrad, o_igrad, sems.at[5]))
+    stores[-1].start()
+    loads[2].wait()
+    stores.append(pltpu.make_async_copy(v_mapped, o_mapped, sems.at[6]))
+    stores[-1].start()
+    for copy in stores:
         copy.wait()
 
 
 def shards(frames, bounds, destinations, kernel, norm_gain, norm_shift, panel, cotangent):
-    idx, flags = routing(destinations, lax.axis_index("dp"))
     hbm = pl.BlockSpec(memory_space=pl.ANY)
     vmem = pl.BlockSpec(memory_space=pltpu.VMEM)
+    smem = pl.BlockSpec(memory_space=pltpu.SMEM)
     shape = jax.ShapeDtypeStruct
+    idx, flags = pl.pallas_call(
+        routing,
+        out_shape=(shape((96,), jnp.int32), shape((40, 128), F32)),
+        in_specs=[smem],
+        out_specs=(smem, vmem),
+    )(destinations)
     mapped, input_grad, *rest = pl.pallas_call(
         fused,
         out_shape=(
@@ -871,9 +922,15 @@
             shape((TAPS, D), F32),
             shape((2, D), F32),
         ),
-        in_specs=[hbm, hbm, vmem, hbm, hbm],
-        out_specs=(hbm, hbm, vmem, hbm, hbm),
-        scratch_shapes=[pltpu.SemaphoreType.DMA((4,))],
+        in_specs=[hbm, hbm, hbm, vmem, vmem],
+        out_specs=(hbm, hbm, hbm, vmem, vmem),
+        scratch_shapes=[
+            pltpu.VMEM((ROWS, D), BF16),
+            pltpu.VMEM((32, 16, D), BF16),
+            pltpu.VMEM((2, 8, 128, 256), BF16),
+            pltpu.VMEM((256, D), F32),
+            pltpu.SemaphoreType.DMA((7,)),
+        ],
         compiler_params=pltpu.CompilerParams(vmem_limit_bytes=60 * 1024 * 1024),
     )(*results)
     return (mapped, input_grad.reshape(SLOTS, D), *rest)

time: 284 us -> 168 us (0.59)
  Pallas kernels: 277 us -> 167 us
  other arithmetic: 3.44 us -> 0 us
    pallas_call x1, Pallas kernels: 119 us -> 5.44 us  [shards(): pl.pallas_call(finish, out_shape=(shape((ROWS, D), BF16), shape((32, 16,...]
    pallas_call x0 -> x1, Pallas kernels: none -> 4.12 us  [shards(): pl.pallas_call(routing, out_shape=(shape((96,), jnp.int32), shape((40, 12...]
where the time goes in v4:
time: 168 us
  Pallas kernels  167 us (99%)
    pallas_call x1, Pallas kernels, shards(): pl.pallas_call(fused, out_shape=(shape((ROWS, D), BF16), shape((32, 16, D...  157 us
    pallas_call x1, Pallas kernels, shards(): pl.pallas_call(finish, out_shape=(shape((ROWS, D), BF16), shape((32, 16,...  5.44 us
    pallas_call x1, Pallas kernels, shards(): pl.pallas_call(routing, out_shape=(shape((96,), jnp.int32), shape((40, 12...  4.12 us

profile of v4, /device:TPU:1, one launch (start us, length us, event | category | flops | bytes accessed | tf_op | source)
XLA Modules:
  0.0 167.6 jit_solution(1905703998240798351)
XLA Ops:
  0.6 4.1 %shard_map.119 = (s32[96]{0:T(128)}, f32[40,128]{1,0:T(8,128)}) custom-call(s32[16,1,16]{2,1,0:T(1,128)} %dest.1), custom_call_target="tpu_custom_call" | custom-call | tf_op jit(solution)/shard_map/pallas_call | solution.py:841
  4.8 157.4 %shard_map.120 = (bf16[384,2048]{1,0:T(8,128)(2,1)}, bf16[32,16,2048]{2,1,0:T(8,128)(2,1)}, bf16[2,8,128,256]{3,2,1,0:T(8,128)(2,1)}, f32[9,2048]{1,0:T(8,128)}, f32[2,2048]{1,0:T(2,128)}) custom-call(s32[96]{0:T(128)} %get-tuple-element.17.idx, f32[40,128]{1,0:T(8,128)} %get-tuple-element.18.flags, s32[2,512]{1,0:T(2,128)} %bounds.1, ...), custom_call_target="tpu_custom_call" | custom-call | tf_op jit(solution)/shard_map/pallas_call | solution.py:847
  162.2 5.4 %shard_map.121 = (bf16[384,2048]{1,0:T(8,128)(2,1)}, bf16[32,16,2048]{2,1,0:T(8,128)(2,1)}, f32[256,2048]{1,0:T(8,128)}, f32[9,2048]{1,0:T(8,128)}, f32[2,2048]{1,0:T(2,128)}) custom-call(bf16[384,2048]{1,0:T(8,128)(2,1)} %get-tuple-element.19.mapped, bf16[32,16,2048]{2,1,0:T(8,128)(2,1)} %get-tuple-element.20.igrad, ...), custom_call_target="tpu_custom_call" | custom-call | tf_op jit(solution)/shard_map/pallas_call | solution.py:916

commit v5 on v4

--- a/solution.py
+++ b/solution.py
@@ -309,7 +309,6 @@
         taps = kern[:, lanes(j)]
         loop(8, lambda i: conv_at(j, pl.multiple_of(i * 64, 64), 64, taps))
 
-    loop(CHUNKS, conv)
 
     load_cot.wait()
     load_panel.wait()
@@ -339,6 +338,8 @@
     loop(8, lambda m: send_cot(same_z(m)), 1)
 
     loop(8, lambda m: send_cot(other_z(m)))
+
+    loop(CHUNKS, conv)
 
     halo_next.wait_recv()
     halo_prev.wait_recv()

time: 168 us -> 163 us (0.970)
  Pallas kernels: 167 us -> 162 us
    pallas_call x1, Pallas kernels: 157 us -> 153 us  [shards(): pl.pallas_call(fused, out_shape=(shape((ROWS, D), BF16), shape((32, 16, D...]
where the time goes in v5:
time: 163 us
  Pallas kernels  162 us (99%)
    pallas_call x1, Pallas kernels, shards(): pl.pallas_call(fused, out_shape=(shape((ROWS, D), BF16), shape((32, 16, D...  153 us
    pallas_call x1, Pallas kernels, shards(): pl.pallas_call(finish, out_shape=(shape((ROWS, D), BF16), shape((32, 16,...  5.44 us
    pallas_call x1, Pallas kernels, shards(): pl.pallas_call(routing, out_shape=(shape((96,), jnp.int32), shape((40, 12...  4.12 us

profile of v5, /device:TPU:1, one launch (start us, length us, event | category | flops | bytes accessed | tf_op | source)
XLA Modules:
  0.0 163.0 jit_solution(3047984185980632517)
XLA Ops:
  0.6 4.1 %shard_map.119 = (s32[96]{0:T(128)}, f32[40,128]{1,0:T(8,128)}) custom-call(s32[16,1,16]{2,1,0:T(1,128)} %dest.1), custom_call_target="tpu_custom_call" | custom-call | tf_op jit(solution)/shard_map/pallas_call | solution.py:842
  4.8 152.8 %shard_map.120 = (bf16[384,2048]{1,0:T(8,128)(2,1)}, bf16[32,16,2048]{2,1,0:T(8,128)(2,1)}, bf16[2,8,128,256]{3,2,1,0:T(8,128)(2,1)}, f32[9,2048]{1,0:T(8,128)}, f32[2,2048]{1,0:T(2,128)}) custom-call(s32[96]{0:T(128)} %get-tuple-element.17.idx, f32[40,128]{1,0:T(8,128)} %get-tuple-element.18.flags, s32[2,512]{1,0:T(2,128)} %bounds.1, ...), custom_call_target="tpu_custom_call" | custom-call | tf_op jit(solution)/shard_map/pallas_call | solution.py:848
  157.6 5.4 %shard_map.121 = (bf16[384,2048]{1,0:T(8,128)(2,1)}, bf16[32,16,2048]{2,1,0:T(8,128)(2,1)}, f32[256,2048]{1,0:T(8,128)}, f32[9,2048]{1,0:T(8,128)}, f32[2,2048]{1,0:T(2,128)}) custom-call(bf16[384,2048]{1,0:T(8,128)(2,1)} %get-tuple-element.19.mapped, bf16[32,16,2048]{2,1,0:T(8,128)(2,1)} %get-tuple-element.20.igrad, ...), custom_call_target="tpu_custom_call" | custom-call | tf_op jit(solution)/shard_map/pallas_call | solution.py:917

commit v6 on v5

--- a/solution.py
+++ b/solution.py
@@ -337,9 +337,14 @@
     cr[0] = cot[idx[RANK]]
     loop(8, lambda m: send_cot(same_z(m)), 1)
 
+
+    loop(CHUNKS, conv)
+
+    own_copies[0].wait_recv()
+    fwd_copies[0].start()
+    fwd_copies[1].start()
+    pair_copies[0].start()
     loop(8, lambda m: send_cot(other_z(m)))
-
-    loop(CHUNKS, conv)
 
     halo_next.wait_recv()
     halo_prev.wait_recv()
@@ -433,10 +438,6 @@
     copy_st2 = over_dp(st2, S_ST2)
     begin(copy_st1, N_FSDP)
 
-    own_copies[0].wait_recv()
-    fwd_copies[0].start()
-    fwd_copies[1].start()
-    pair_copies[0].start()
     own_copies[1].wait_recv()
     far_copies[0].start()
     pair_copies[1].start()

time: 163 us -> 166 us (1.018)
  Pallas kernels: 162 us -> 164 us
    pallas_call x1, Pallas kernels: 153 us -> 155 us  [shards(): pl.pallas_call(fused, out_shape=(shape((ROWS, D), BF16), shape((32, 16, D...]
where the time goes in v6:
time: 166 us; the launch traced here: 165 us
  Pallas kernels  164 us (99%)
    pallas_call x1, Pallas kernels, shards(): pl.pallas_call(fused, out_shape=(shape((ROWS, D), BF16), shape((32, 16, D...  155 us
    pallas_call x1, Pallas kernels, shards(): pl.pallas_call(finish, out_shape=(shape((ROWS, D), BF16), shape((32, 16,...  5.44 us
    pallas_call x1, Pallas kernels, shards(): pl.pallas_call(routing, out_shape=(shape((96,), jnp.int32), shape((40, 12...  4.12 us

profile of v6, /device:TPU:1, one launch (start us, length us, event | category | flops | bytes accessed | tf_op | source)
XLA Modules:
  0.0 165.0 jit_solution(16610611144237989334)
XLA Ops:
  0.6 4.1 %shard_map.119 = (s32[96]{0:T(128)}, f32[40,128]{1,0:T(8,128)}) custom-call(s32[16,1,16]{2,1,0:T(1,128)} %dest.1), custom_call_target="tpu_custom_call" | custom-call | tf_op jit(solution)/shard_map/pallas_call | solution.py:843
  4.8 154.8 %shard_map.120 = (bf16[384,2048]{1,0:T(8,128)(2,1)}, bf16[32,16,2048]{2,1,0:T(8,128)(2,1)}, bf16[2,8,128,256]{3,2,1,0:T(8,128)(2,1)}, f32[9,2048]{1,0:T(8,128)}, f32[2,2048]{1,0:T(2,128)}) custom-call(s32[96]{0:T(128)} %get-tuple-element.17.idx, f32[40,128]{1,0:T(8,128)} %get-tuple-element.18.flags, s32[2,512]{1,0:T(2,128)} %bounds.1, ...), custom_call_target="tpu_custom_call" | custom-call | tf_op jit(solution)/shard_map/pallas_call | solution.py:849
  159.5 5.4 %shard_map.121 = (bf16[384,2048]{1,0:T(8,128)(2,1)}, bf16[32,16,2048]{2,1,0:T(8,128)(2,1)}, f32[256,2048]{1,0:T(8,128)}, f32[9,2048]{1,0:T(8,128)}, f32[2,2048]{1,0:T(2,128)}) custom-call(bf16[384,2048]{1,0:T(8,128)(2,1)} %get-tuple-element.19.mapped, bf16[32,16,2048]{2,1,0:T(8,128)(2,1)} %get-tuple-element.20.igrad, ...), custom_call_target="tpu_custom_call" | custom-call | tf_op jit(solution)/shard_map/pallas_call | solution.py:918
